TPU v7x, 512 devices: a whole 4x8x8 slice. The times are simulated.
512 devices in a mesh: layer: 32 (over x_hi, y, core), lat: 16 (over x_lo, z).
Axes of the slice: x: 4 (x_hi: 2, x_lo: 2; x = x_hi * 2 + x_lo), y: 8, z: 8, core: 2. Of those that a mesh axis runs over, the one named last changes fastest.
Arguments:
- layer_inputs: bfloat16 [4, 3584, 704], P(None, 'lat', 'layer'), may hold values from -6 to 6
- layer_outputs: bfloat16 [704, 4, 3584], P('layer', None, 'lat'), may hold values from -6 to 6
- encoder: bfloat16 [4, 3584, 8192], P(None, 'lat', 'layer'), may hold values from -0.09375 to 0.09375
- encoder_bias: float32 [4, 8192], P(None, 'layer'), may hold values from -3 to 3
- decoder: bfloat16 [10, 3584, 8192], P(None, 'lat', 'layer'), may hold values from -0.1875 to 0.1875
- active_blocks: int32 [4, 22, 8], replicated, may hold values from 0 to 63, all different within a row; in each aligned block of 22 rows (0 to 21, 22 to 43, ..., all dimensions but the last counted through in order) at most 4 rows name the same one
Outputs:
- reconstruction: bfloat16 [704, 4, 3584], P('layer', None, 'lat')
- encoder_grad: bfloat16 [4, 3584, 8192], P(None, 'lat', 'layer')
- bias_grad: float32 [4, 8192], P(None, 'layer')
- decoder_grad: bfloat16 [10, 3584, 8192], P(None, 'lat', 'layer')
Inputs may be any that keep to these rules, and one draw needn't show every extreme that they name: `active_blocks`: each list names 8 different latent blocks, and every block is named in some list. Among the 22 lists of one layer, no block is named by more than 4 lists, and in every draw some block of some layer is named by exactly 4.
All inputs are finite; a program needn't handle non-finite values.
Results may differ from a plain program's by a relative error of at most 0.0058.
Values may be sent and summed in bfloat16 or wider, within the bound.
A program may use at most 64 MiB of HBM per device.

v0:
```python
import jax
import jax.numpy as jnp
from jax import lax
from jax.sharding import PartitionSpec as P

BLOCK = 128
ROWBLOCK = 32
NBLOCKS = 64


def block_mask(active_blocks, lat_first, lat_count, row_total):
    onehot = jnp.any(
        active_blocks[:, :, :, None] == jnp.arange(NBLOCKS, dtype=jnp.int32)[None, None, None, :],
        axis=2,
    )
    row_block = jnp.arange(row_total, dtype=jnp.int32) // ROWBLOCK
    lat_block = (lat_first + jnp.arange(lat_count, dtype=jnp.int32)) // BLOCK
    picked = jnp.take(onehot, row_block, axis=1)
    picked = jnp.take(picked, lat_block, axis=2)
    return jnp.transpose(picked, (0, 2, 1)).astype(jnp.float32)


def contract(left, right, left_dim, right_dim):
    return lax.dot_general(
        left.astype(jnp.float32),
        right.astype(jnp.float32),
        (((left_dim,), (right_dim,)), ((), ())),
        preferred_element_type=jnp.float32,
    )


def decode_rows(decoder, latent_codes, row_count):
    layers = latent_codes.shape[0]
    outputs = []
    for target in range(layers):
        pair_first = target * (target + 1) // 2
        accum = contract(latent_codes[0], decoder[pair_first], 0, 1)
        for source in range(1, target + 1):
            accum = accum + contract(latent_codes[source], decoder[pair_first + source], 0, 1)
        outputs.append(accum)
    return jnp.stack(outputs, axis=1).reshape(row_count, -1)


def local(layer_inputs, layer_outputs, encoder, encoder_bias, decoder, active_blocks):
    layers, dim_local, lat_local = encoder.shape
    rows_local = layer_outputs.shape[0]
    inputs_all = lax.all_gather(layer_inputs, "layer", axis=2, tiled=True)
    row_total = inputs_all.shape[2]
    lat_first = lax.axis_index("layer") * lat_local
    pre_part = jnp.stack(
        [contract(encoder[source], inputs_all[source], 0, 0) for source in range(layers)]
    )
    live_mask = block_mask(active_blocks, lat_first, lat_local, row_total)
    pre_total = lax.psum(pre_part, "lat") + encoder_bias[:, :, None]
    latent_codes = (live_mask * jax.nn.softplus(pre_total)).astype(jnp.bfloat16)
    slope_vals = live_mask * jax.nn.sigmoid(pre_total)
    recon_local = lax.psum_scatter(
        decode_rows(decoder, latent_codes, rows_local * lax.axis_size("layer")),
        "layer",
        scatter_dimension=0,
        tiled=True,
    ).reshape(rows_local, layers, dim_local)
    error_local = (recon_local - layer_outputs.astype(jnp.float32)).astype(jnp.bfloat16)
    error_all = lax.all_gather(error_local, "layer", axis=0, tiled=True)
    grad_pieces = []
    grad_lists = [None] * layers
    for target in range(layers):
        pair_first = target * (target + 1) // 2
        error_slab = error_all[:, target, :]
        for source in range(target + 1):
            grad_pieces.append(
                contract(error_slab, latent_codes[source], 0, 1).astype(jnp.bfloat16)
            )
            back_term = contract(decoder[pair_first + source], error_slab, 0, 1)
            grad_lists[source] = (
                back_term if grad_lists[source] is None else grad_lists[source] + back_term
            )
    decoder_grad = jnp.stack(grad_pieces)
    code_grad = jnp.stack(grad_lists)
    pre_grad = (lax.psum(code_grad, "lat") * slope_vals).astype(jnp.bfloat16)
    encoder_grad = jnp.stack(
        [
            contract(inputs_all[source], pre_grad[source], 1, 1).astype(jnp.bfloat16)
            for source in range(layers)
        ]
    )
    bias_grad = jnp.sum(pre_grad.astype(jnp.float32), axis=2)
    return (recon_local.astype(jnp.bfloat16), encoder_grad, bias_grad, decoder_grad)


def solution(mesh):
    placed = (
        P(None, "lat", "layer"),
        P("layer", None, "lat"),
        P(None, "lat", "layer"),
        P(None, "layer"),
        P(None, "lat", "layer"),
        P(),
    )
    return jax.shard_map(
        local,
        mesh=mesh,
        in_specs=placed,
        out_specs=(
            P("layer", None, "lat"),
            P(None, "lat", "layer"),
            P(None, "layer"),
            P(None, "lat", "layer"),
        ),
        check_vma=False,
    )
```

profile of v0, /device:TPU:1, one launch (start us, length us, event | category | flops | bytes accessed | tf_op | source)
XLA Modules:
  0.0 808.8 jit_solution(17045939864665002867)
XLA Ops:
  7.2 0.7 all-gather.3.cloned.1.call-update
  7.9 93.2 %all-gather.3.cloned.1.call-done = bf16[4,224,704]{1,0,2:T(4,128)(2,1)} async-done(((bf16[4,224,22]{1,0,2:T(4,128)(2,1)}), bf16[4,224,704]{1,0,2:T(4,128)(2,1)}) %all-gather.3.cloned.1.call-update) | async-done | bytes 1261584 | tf_op jit(solution)/shard_map/all_gather | solution.py:47
  101.1 5.6 fusion.123
  106.7 0.8 copy.50
  107.5 1.8 copy.49
  109.3 1.2 convolution_bitcast_fusion.1
  110.5 1.4 convolution_bitcast_fusion.2
  111.9 0.8 copy.48
  112.7 1.3 convolution_bitcast_fusion.3
  114.0 1.8 copy.47
  115.8 1.4 convolution_bitcast_fusion.4
  117.2 1.9 pad_maximum_fusion
  119.3 0.5 copy-done.10
  120.2 2.8 gather_fusion
  123.0 2.6 select_bitcast_fusion
  125.6 1.2 copy.33
  126.9 2.3 gather_fusion.1
  129.2 1.7 copy.34
  131.0 126.2 %all-reduce.5.cloned.1.call-done = f32[4,256,704]{1,2,0:T(8,128)} async-done(((f32[4,256,704]{1,2,0:T(8,128)}), f32[4,256,704]{1,2,0:T(8,128)}) %all-reduce.5.cloned.1.call-update) | async-done | bytes 2883600 | tf_op jit(solution)/shard_map/psum | solution.py:54
  257.2 3.8 fusion.1
  263.9 1.8 pad_maximum_fusion.2
  265.8 1.3 dynamic-slice
  267.7 281.4 %all-reduce.9.cloned.1.call-done = f32[704,896]{0,1:T(8,128)} async-done(((f32[704,896]{0,1:T(8,128)}), f32[704,896]{0,1:T(8,128)}) %all-reduce.9.cloned.1.call-update) | async-done | bytes 2523152
  549.1 1.4 constant_dynamic-slice_fusion
  550.7 0.7 subtract_convert_fusion
  551.7 85.3 %all-gather.5.cloned.1.call-done = bf16[704,4,224]{2,1,0:T(4,128)(2,1)} async-done(((bf16[22,4,224]{2,1,0:T(4,128)(2,1)}), bf16[704,4,224]{2,1,0:T(4,128)(2,1)}) %all-gather.5.cloned.1.call-update) | async-done | bytes 1261584 | tf_op jit(solution)/shard_map/all_gather | solution.py:64
  636.9 6.5 fusion.122
  643.5 0.7 copy.51
  644.2 2.2 copy.52
  646.4 2.2 copy.53
  648.6 2.2 copy.54
  650.7 1.3 fusion.54
  652.0 1.2 fusion.50
  655.8 1.9 pad_maximum_fusion.1
  657.7 0.9 fusion.9
  658.6 0.9 fusion.11
  659.6 0.9 fusion.13
  660.5 0.9 fusion.15
  661.4 0.9 fusion.17
  662.3 0.9 fusion.19
  663.2 0.9 fusion.21
  664.1 0.9 fusion.23
  665.0 0.9 fusion.25
  665.9 0.9 fusion.27
  666.8 128.7 %all-reduce.7.cloned.1.call-done = f32[4,256,704]{1,2,0:T(8,128)} async-done(((f32[4,256,704]{1,2,0:T(8,128)}), f32[4,256,704]{1,2,0:T(8,128)}) %all-reduce.7.cloned.1.call-update) | async-done | bytes 2883600 | tf_op jit(solution)/shard_map/psum | solution.py:80
  795.6 4.4 convert_reduce_fusion
  800.5 0.4 copy-done.4
  801.4 0.8 pad_maximum_fusion.3
  (60 shorter events, 7.7 us)
Async XLA Ops:
  7.2 94.0 %all-gather.3.cloned.1.call-start = ((), (), s32[]{:S(2)}) async-start(), calls=%async_computation | async-start | bytes 1486848 | tf_op jit(solution)/shard_map/all_gather | solution.py:47
  7.9 249.3 %all-reduce.5.cloned.1.call-start = ((), (), s32[]{:S(2)}) async-start(), calls=%async_computation.1 | async-start | bytes 5767168 | tf_op jit(solution)/shard_map/psum | solution.py:54
  107.5 4.4 copy-start.2
  112.7 4.5 copy-start.5
  119.1 0.7 copy-start.10
  119.1 430.0 %all-reduce.9.cloned.1.call-start = ((), (), s32[]{:S(2)}) async-start(), calls=%async_computation.4 | async-start | bytes 5505024
  126.9 130.3 %copy-start.9 = (f32[4,256]{1,0:T(4,128)S(1)}, f32[4,256]{1,0:T(4,128)}, u32[]{:S(2)}) copy-start(f32[4,256]{1,0:T(4,128)} %param.9) | copy-start | bytes 12292
  131.0 130.1 %copy-start = (bf16[10,224,256]{2,1,0:T(8,128)(2,1)S(1)}, bf16[10,224,256]{2,1,0:T(8,128)(2,1)}, u32[]{:S(2)}) copy-start(bf16[10,224,256]{2,1,0:T(8,128)(2,1)} %param.10) | copy-start | bytes 3440644
  265.7 285.0 %copy-start.8 = (bf16[22,4,224]{2,1,0:T(4,128)(2,1)S(1)}, bf16[22,4,224]{2,1,0:T(4,128)(2,1)}, u32[]{:S(2)}) copy-start(bf16[22,4,224]{2,1,0:T(4,128)(2,1)} %param.7) | copy-start | bytes 118276
  265.7 371.2 %all-gather.5.cloned.1.call-start = ((), (), s32[]{:S(2)}) async-start(), calls=%async_computation.2 | async-start | bytes 1486848 | tf_op jit(solution)/shard_map/all_gather | solution.py:64
  551.4 244.2 %all-reduce.7.cloned.1.call-start = ((), (), s32[]{:S(2)}) async-start(), calls=%async_computation.3 | async-start | bytes 5767168 | tf_op jit(solution)/shard_map/psum | solution.py:80
  650.7 2.5 copy-start.1
  666.8 133.1 %copy-start.7 = (bf16[1,224,704]{2,1,0:T(8,128)(2,1)S(1)}, bf16[1,224,704]{2,1,0:T(8,128)(2,1)}, u32[]{:S(2)}) copy-start(bf16[1,224,704]{2,1,0:T(8,128)(2,1)} %copy.47) | copy-start | bytes 946180
  666.8 133.4 %copy-start.6 = (bf16[1,224,704]{2,1,0:T(8,128)(2,1)S(1)}, bf16[1,224,704]{2,1,0:T(8,128)(2,1)}, u32[]{:S(2)}) copy-start(bf16[1,224,704]{2,1,0:T(8,128)(2,1)} %copy-done.5) | copy-start | bytes 946180
  799.9 1.0 copy-start.4
  799.9 1.2 copy-start.3
Sparse Core Ops, SparseCore 0:
  11.3 89.7 all-gather.2
  119.2 137.9 all-reduce.4
  265.8 283.2 all-reduce.8
  552.8 84.0 all-gather.4
  657.9 137.6 all-reduce.6
where the time goes:
time: 819 us; the launch traced here: 809 us
  waiting for transfers between devices  716 us (87%)
  local copies, waits for them, and re-layouts  36.5 us (4%)
  matrix products  23.2 us (3%)
  other arithmetic  18 us (2%)
  between operations  14.9 us (2%)
    unnamed x6, waiting for transfers between devices  282 us
    psum x1, waiting for transfers between devices, local(): pre_grad = (lax.psum(code_grad, 'lat') * slope_vals).astype(jnp.bfloat16)  129 us
    psum x1, waiting for transfers between devices, local(): pre_total = lax.psum(pre_part, 'lat') + encoder_bias[:, :, None]  126 us
    all_gather x1, waiting for transfers between devices, local(): inputs_all = lax.all_gather(layer_inputs, 'layer', axis=2, tiled=True)  93.2 us
    all_gather x1, waiting for transfers between devices, local(): error_all = lax.all_gather(error_local, 'layer', axis=0, tiled=True)  85.3 us
    dot_general x38, matrix products, contract(): lax.dot_general(left.astype(jnp.float32), right.astype(jnp.float32), (((l...  23.2 us
  transfers between devices with their start and end apart: 5, of which 5 were waited for; matrix products, arithmetic and copies ran while one was open for 3% of the time, Pallas kernels for 0%

commit v1 on v0

v1 whole, which is shorter than its diff:
```python
import functools

import jax
import jax.numpy as jnp
from jax import lax
from jax.experimental import pallas as pl
from jax.experimental.pallas import tpu as pltpu
from jax.sharding import PartitionSpec as P

BLOCK = 128
ROWBLOCK = 32
MOST = 4
SLOTS = MOST * ROWBLOCK
LANE = 128
BF, F32 = jnp.bfloat16, jnp.float32


def dot(a, b, dims=((1,), (0,))):
    return lax.dot_general(a, b, (dims, ((), ())), preferred_element_type=F32)


def iota(shape, dim):
    return lax.broadcasted_iota(jnp.int32, shape, dim)


def kernel(
    sizes,
    x_ref, y_ref, enc_ref, bias_ref, dec_ref, act_ref,
    rec_ref, eg_ref, bg_ref, dg_ref,
    xg, eg, xt, et, cd, pgd, encp, dcat, sel, selt,
    xy_s, xy_r, pk, rx, ck, pc, rc, pg, slope,
    hm_s, hm_r, ho, ra_s, ra_r, rb_s, rb_r, fx_s, fx_r, recb,
    load_sem, xy_sem, ag_x, ag_as, ag_ar, ag_bs, ag_br, ag_ms, ag_mr,
    lat_s, lat_r, hm_sem, rs_as, rs_ar, rs_bs, rs_br, fx_sem, rec_sem,
):
    layers, dl, lats, rows, ny, nl, chunk = sizes
    width = layers * dl
    span = 3 * LANE
    half = ny * chunk
    places = 2 * half
    real = 2 * rows
    shard = 2 * SLOTS // nl
    na, nb = ny // 2, ny // 2 - 1

    me, q = lax.axis_index("layer"), lax.axis_index("lat")
    core = lax.rem(me, 2)
    y = lax.rem(me // 2, ny)
    h = me // (2 * ny)
    owner = core == h
    step = 1 - 2 * core

    def at(hh, yy, cc):
        return {"layer": (hh * ny + yy) * 2 + cc, "lat": q}

    mate, partner = at(h, y, 1 - core), at(1 - h, y, core)
    y_a, y_b = lax.rem(y + step + ny, ny), lax.rem(y - step + ny, ny)
    to_a, to_b = at(h, y_a, core), at(h, y_b, core)

    def place(hh, offset):
        slot = lax.rem(y + step * offset + 2 * ny, ny)
        return pl.ds(pl.multiple_of((hh * ny + slot) * chunk, 16), chunk)

    def local(offset):
        return place(0, offset)

    barrier = pltpu.get_barrier_semaphore()
    for peer in (mate, partner, to_a, to_b):
        pl.semaphore_signal(barrier, inc=1, device_id=peer)

    def greet(d, carry):
        pl.semaphore_signal(barrier, inc=1, device_id={"layer": me, "lat": lax.rem(q + d, nl)})
        return carry

    lax.fori_loop(1, nl, greet, 0)
    pl.semaphore_wait(barrier, 4 + nl - 1)

    put = jnp.where(iota((chunk, rows), 0) == iota((chunk, rows), 1) + rows * core, 1.0, 0.0).astype(BF)
    xy_s[0:chunk, :] = dot(put, x_ref[...].reshape(width, rows), ((1,), (1,))).astype(BF)
    xy_s[chunk : 2 * chunk, :] = dot(put, y_ref[...]).astype(BF)
    xy_copy = pltpu.make_async_remote_copy(xy_s, xy_r, xy_sem.at[0], xy_sem.at[1], device_id=mate)
    xy_copy.start()

    encp[...] = jnp.zeros_like(encp)
    dcat[...] = jnp.zeros_like(dcat)
    loads = []

    def first(s):
        return min(dl * s // LANE * LANE, width - span)

    for s in range(layers):
        loads.append(pltpu.make_async_copy(enc_ref.at[s], encp.at[s, pl.ds(dl * s - first(s), dl)], load_sem.at[s]))
    for t in range(layers):
        for s in range(t + 1):
            pair = t * (t + 1) // 2 + s
            loads.append(
                pltpu.make_async_copy(
                    dec_ref.at[pair], dcat.at[pl.ds(dl * t, dl), pl.ds(lats * s, lats)], load_sem.at[layers + pair]
                )
            )
    for copy in loads:
        copy.start()

    xy_copy.wait_recv()
    xg_own = place(core, 0)

    def gather_copies(buf, n):
        def ring(to, offset, send, recv):
            where = buf.at[place(core, offset)]
            return pltpu.make_async_remote_copy(where, where, send, recv, device_id=to)

        cross = ring(partner, 0, ag_x.at[n, 0], ag_x.at[n, 1])
        a_out = [ring(to_a, -i, ag_as.at[n, i], ag_ar.at[n, i]) for i in range(na)]
        b_out = [ring(to_b, i, ag_bs.at[n, i], ag_br.at[n, i]) for i in range(nb)]
        a_in = [ring(to_a, -i - 1, ag_as.at[n, i], ag_ar.at[n, i]) for i in range(na)]
        b_in = [ring(to_b, i + 1, ag_bs.at[n, i], ag_br.at[n, i]) for i in range(nb)]
        order = [0]
        for i in range(na):
            order.append(-i - 1)
            if i < nb:
                order.append(i + 1)
        pass_on = [ring(mate, o, ag_ms.at[n, j], ag_mr.at[n, j]) for j, o in enumerate(order)]
        from_mate = []
        for j, o in enumerate(order):
            where = buf.at[place(1 - core, -o)]
            from_mate.append(pltpu.make_async_remote_copy(where, where, ag_ms.at[n, j], ag_mr.at[n, j], device_id=mate))
        return cross, a_out, b_out, a_in, b_in, pass_on, from_mate

    def gather_start(copies):
        cross, a_out, b_out, a_in, b_in, pass_on, from_mate = copies

        @pl.when(owner)
        def _():
            cross.start()

        @pl.when(jnp.logical_not(owner))
        def _():
            cross.wait_recv()

        a_out[0].start()
        if nb:
            b_out[0].start()
        pass_on[0].start()

    def gather_run(copies):
        cross, a_out, b_out, a_in, b_in, pass_on, from_mate = copies
        j = 1
        for i in range(na):
            a_in[i].wait_recv()
            if i + 1 < na:
                a_out[i + 1].start()
            pass_on[j].start()
            j += 1
            if i < nb:
                b_in[i].wait_recv()
                if i + 1 < nb:
                    b_out[i + 1].start()
                pass_on[j].start()
                j += 1
        for copy in from_mate:
            copy.wait_recv()

    def gather_end(copies):
        cross, a_out, b_out, a_in, b_in, pass_on, from_mate = copies

        @pl.when(owner)
        def _():
            cross.wait_send()

        for copy in a_out + b_out + pass_on:
            copy.wait_send()

    x_copies = gather_copies(xg, 0)

    @pl.when(owner)
    def _():
        xg[xg_own, :] = xy_s[0:chunk, :] + xy_r[0:chunk, :]

    gather_start(x_copies)

    nr = act_ref.shape[1]
    ii, jj = iota((nr, nr), 0), iota((nr, nr), 1)
    lane_place = iota((1, places), 1)
    lane_chip = jnp.zeros((1, places), jnp.int32)
    for c in range(1, 2 * ny):
        lane_chip = lane_chip + jnp.where(lane_place >= c * chunk, 1, 0)
    lane_in = lane_place - lane_chip * chunk
    lane_row = jnp.where(lane_in < real, lane_chip * real + lane_in, -2).astype(F32)
    m0, r1 = iota((SLOTS, nr), 0), iota((SLOTS, nr), 1)
    r0, m1 = iota((nr, SLOTS), 0), iota((nr, SLOTS), 1)
    col_rank = (m0 // ROWBLOCK).astype(F32)
    col_value = (ROWBLOCK * r1 + m0 % ROWBLOCK + 1).astype(F32)
    row_rank = (m1 // ROWBLOCK).astype(F32)
    row_value = (ROWBLOCK * r0 + m1 % ROWBLOCK + 1).astype(F32)
    chip_in = iota((chunk, SLOTS), 0)

    def choose(s, carry):
        named = act_ref[s]
        for b in range(2):
            hit = jnp.max(jnp.where(named == 2 * me + b, 1.0, 0.0), axis=1, keepdims=True)
            across = jnp.broadcast_to(hit, (nr, nr))
            hit_row = jnp.sum(jnp.where(ii == jj, across, 0.0), axis=0, keepdims=True)
            rank_row = jnp.sum(jnp.where(ii < jj, across, 0.0), axis=0, keepdims=True)
            rank = jnp.sum(jnp.where(jj < ii, jnp.broadcast_to(hit_row, (nr, nr)), 0.0), axis=1, keepdims=True)
            rank_row = jnp.where(hit_row > 0, rank_row, -1.0)
            rank = jnp.where(hit > 0, rank, -1.0)
            want = jnp.sum(jnp.where(rank_row == col_rank, col_value, 0.0), axis=1, keepdims=True) - 1.0
            want_row = jnp.sum(jnp.where(rank == row_rank, row_value, 0.0), axis=0, keepdims=True) - 1.0
            sel[s, b * SLOTS : (b + 1) * SLOTS, :] = jnp.where(want == lane_row, 1.0, 0.0).astype(BF)
            for c in range(2 * ny):
                row = jnp.where(chip_in < real, chip_in + c * real, -2).astype(F32)
                selt[s, c * chunk : (c + 1) * chunk, b * SLOTS : (b + 1) * SLOTS] = jnp.where(
                    row == want_row, 1.0, 0.0
                ).astype(BF)
        return carry

    lax.fori_loop(0, layers, choose, 0)

    gather_run(x_copies)
    for copy in loads[:layers]:
        copy.wait()

    def lat_rows(j):
        return pl.ds(pl.multiple_of(j * shard, 16), shard)

    def scatter(src, dst, s, n):
        def one(d, carry):
            peer = lax.rem(q + d, nl)
            pltpu.make_async_remote_copy(
                src.at[s, lat_rows(peer)], dst.at[s, q], lat_s.at[n, s], lat_r.at[n, s],
                device_id={"layer": me, "lat": peer},
            ).start()
            return carry

        lax.fori_loop(1, nl, one, 0)
        dst[s, q] = src[s, lat_rows(q), :]

    def spread(buf, s, n):
        def one(d, carry):
            where = buf.at[s, lat_rows(q)]
            pltpu.make_async_remote_copy(
                where, where, lat_s.at[n, s], lat_r.at[n, s], device_id={"layer": me, "lat": lax.rem(q + d, nl)}
            ).start()
            return carry

        lax.fori_loop(1, nl, one, 0)

    def lat_wait(sem, s, n):
        where = ck.at[s, pl.ds(0, (nl - 1) * shard)]
        pltpu.make_async_copy(where, where, sem.at[n, s]).wait()

    def pack(dense, dst, s):
        both = dot(sel[s], dense)
        for b in range(2):
            part = slice(b * SLOTS, (b + 1) * SLOTS)
            dst[s, part, :] = both[part, b * BLOCK : (b + 1) * BLOCK].astype(BF)

    for s in range(layers):
        dense = dot(xg[:, first(s) : first(s) + span], encp[s]).astype(BF)
        pack(dense, pk, s)
        scatter(pk, rx, s, 0)

    for n in range(width // LANE):
        xt[n * LANE : (n + 1) * LANE, :] = xg[:, n * LANE : (n + 1) * LANE].T

    b_of = q * shard // SLOTS
    for s in range(layers):
        lat_wait(lat_r, s, 0)
        total = jnp.sum(rx[s].astype(F32), axis=0)
        bias = jnp.where(b_of == 0, bias_ref[s : s + 1, 0:BLOCK], bias_ref[s : s + 1, BLOCK : 2 * BLOCK])
        pre = total + bias
        small = jnp.exp(-jnp.abs(pre))
        ck[s, lat_rows(q), :] = (jnp.maximum(pre, 0.0) + jnp.log1p(small)).astype(BF)
        slope[s] = jnp.where(pre >= 0, 1.0, small) / (1.0 + small)
        spread(ck, s, 1)

    def unpack(src, dst, s):
        zero = jnp.zeros((SLOTS, BLOCK), BF)
        wide = jnp.concatenate(
            [
                jnp.concatenate([src[s, 0:SLOTS, :], zero], axis=1),
                jnp.concatenate([zero, src[s, SLOTS : 2 * SLOTS, :]], axis=1),
            ],
            axis=0,
        )
        dst[:, s * lats : (s + 1) * lats] = dot(selt[s], wide).astype(BF)

    for s in range(layers):
        lat_wait(lat_r, s, 1)
        unpack(ck, cd, s)

    for copy in loads[layers:]:
        copy.wait()

    tiles = [min(layers, ((n + 1) * LANE - 1) // dl + 1) for n in range(width // LANE)]
    groups = []
    for n, count in enumerate(tiles):
        if groups and groups[-1][2] == count:
            groups[-1][1] = n + 1
        else:
            groups.append([n, n + 1, count])

    def decode(hh, out):
        base = pl.ds(pl.multiple_of(hh * half, 16), half)
        for lo, hi, count in groups:
            lanes = slice(lo * LANE, hi * LANE)
            out[:, lanes] = dot(cd[base, 0 : count * lats], dcat[lanes, 0 : count * lats], ((1,), (1,))).astype(out.dtype)

    decode(1 - core, hm_s)
    hm_copy = pltpu.make_async_remote_copy(hm_s, hm_r, hm_sem.at[0], hm_sem.at[1], device_id=mate)
    hm_copy.start()
    decode(core, ho)
    hm_copy.wait_recv()

    def mine(offset):
        return ho[local(offset), :] + hm_r[local(offset), :].astype(F32)

    a_copies = [
        pltpu.make_async_remote_copy(ra_s.at[i], ra_r.at[i], rs_as.at[i], rs_ar.at[i], device_id=to_a) for i in range(na)
    ]
    b_copies = [
        pltpu.make_async_remote_copy(rb_s.at[i], rb_r.at[i], rs_bs.at[i], rs_br.at[i], device_id=to_b) for i in range(nb)
    ]
    for i in range(na):
        part = mine(na - i)
        if i:
            a_copies[i - 1].wait_recv()
            part = part + ra_r[i - 1].astype(F32)
        ra_s[i] = part.astype(BF)
        a_copies[i].start()
        if i < nb:
            part = mine(i - nb)
            if i:
                b_copies[i - 1].wait_recv()
                part = part + rb_r[i - 1].astype(F32)
            rb_s[i] = part.astype(BF)
            b_copies[i].start()
    total = mine(0)
    a_copies[na - 1].wait_recv()
    total = total + ra_r[na - 1].astype(F32)
    if nb:
        b_copies[nb - 1].wait_recv()
        total = total + rb_r[nb - 1].astype(F32)
    ho[local(0), :] = total

    fx_copy = pltpu.make_async_remote_copy(fx_s, fx_r, fx_sem.at[0], fx_sem.at[1], device_id=partner)
    rec_copy = pltpu.make_async_remote_copy(recb, recb, rec_sem.at[0], rec_sem.at[1], device_id=mate)
    e_copies = gather_copies(eg, 1)

    @pl.when(jnp.logical_not(owner))
    def _():
        fx_s[...] = ho[local(0), :].astype(BF)
        fx_copy.start()

    @pl.when(owner)
    def _():
        fx_copy.wait_recv()
        whole = ho[local(0), :] + fx_r[...].astype(F32)
        outs = xy_s[chunk : 2 * chunk, :].astype(F32) + xy_r[chunk : 2 * chunk, :].astype(F32)
        eg[xg_own, :] = (whole - outs).astype(BF)
        recb[...] = whole.astype(BF)

    gather_start(e_copies)

    @pl.when(owner)
    def _():
        rec_copy.start()

    gather_run(e_copies)

    for s in range(layers - 1, -1, -1):
        low = dl * s // LANE * LANE
        dense = dot(eg[:, low:width], dcat[low:width, s * lats : (s + 1) * lats]).astype(BF)
        pack(dense, pc, s)
        scatter(pc, rc, s, 2)

    for n in range(width // LANE):
        et[n * LANE : (n + 1) * LANE, :] = eg[:, n * LANE : (n + 1) * LANE].T

    def decoder_grad(t):
        out = dot(et[t * dl : (t + 1) * dl, :], cd[:, 0 : (t + 1) * lats])
        for s in range(t + 1):
            dg_ref[t * (t + 1) // 2 + s] = out[:, s * lats : (s + 1) * lats].astype(BF)

    decoder_grad(0)
    decoder_grad(1)

    for s in range(layers - 1, -1, -1):
        lat_wait(lat_r, s, 2)
        total = jnp.sum(rc[s].astype(F32), axis=0)
        pg[s, lat_rows(q), :] = (total * slope[s]).astype(BF)
        spread(pg, s, 3)

    decoder_grad(2)
    decoder_grad(3)

    for s in range(layers - 1, -1, -1):
        lat_wait(lat_r, s, 3)
        unpack(pg, pgd, s)
        for b in range(2):
            bg_ref[s : s + 1, b * BLOCK : (b + 1) * BLOCK] = jnp.sum(
                pg[s, b * SLOTS : (b + 1) * SLOTS, :].astype(F32), axis=0, keepdims=True
            )
        eg_ref[s] = dot(xt[s * dl : (s + 1) * dl, :], pgd[:, s * lats : (s + 1) * lats]).astype(BF)

    @pl.when(owner)
    def _():
        rec_copy.wait_send()

    @pl.when(jnp.logical_not(owner))
    def _():
        fx_copy.wait_send()
        rec_copy.wait_recv()

    take = jnp.where(iota((rows, chunk), 1) == iota((rows, chunk), 0) + rows * core, 1.0, 0.0).astype(BF)
    rec_ref[...] = dot(take, recb[...]).astype(BF)

    xy_copy.wait_send()
    hm_copy.wait_send()
    for copy in a_copies + b_copies:
        copy.wait_send()
    gather_end(x_copies)
    gather_end(e_copies)
    for n in range(4):
        for s in range(layers):
            lat_wait(lat_s, s, n)


def step(sizes, layer_inputs, layer_outputs, encoder, encoder_bias, decoder, active_blocks):
    layers, dl, lats, rows, ny, nl, chunk = sizes
    width = layers * dl
    places = 2 * ny * chunk
    na, nb = ny // 2, max(1, ny // 2 - 1)
    shard = 2 * SLOTS // nl
    pairs = decoder.shape[0]
    vmem, dma = pltpu.VMEM, pltpu.SemaphoreType.DMA
    ring = (chunk, width)
    scratch = [
        vmem((places, width), BF),
        vmem((places, width), BF),
        vmem((width, places), BF),
        vmem((width, places), BF),
        vmem((places, layers * lats), BF),
        vmem((places, layers * lats), BF),
        vmem((layers, 3 * LANE, lats), BF),
        vmem((width, layers * lats), BF),
        vmem((layers, 2 * SLOTS, places), BF),
        vmem((layers, places, 2 * SLOTS), BF),
        vmem((2 * chunk, width), BF),
        vmem((2 * chunk, width), BF),
        vmem((layers, 2 * SLOTS, BLOCK), BF),
        vmem((layers, nl, shard, BLOCK), BF),
        vmem((layers, 2 * SLOTS, BLOCK), BF),
        vmem((layers, 2 * SLOTS, BLOCK), BF),
        vmem((layers, nl, shard, BLOCK), BF),
        vmem((layers, 2 * SLOTS, BLOCK), BF),
        vmem((layers, shard, BLOCK), F32),
        vmem((places // 2, width), BF),
        vmem((places // 2, width), BF),
        vmem((places // 2, width), F32),
        vmem((na,) + ring, BF),
        vmem((na,) + ring, BF),
        vmem((nb,) + ring, BF),
        vmem((nb,) + ring, BF),
        vmem(ring, BF),
        vmem(ring, BF),
        vmem(ring, BF),
        dma((layers + pairs,)),
        dma((2,)),
        dma((2, 2)),
        dma((2, na)),
        dma((2, na)),
        dma((2, nb)),
        dma((2, nb)),
        dma((2, ny)),
        dma((2, ny)),
        dma((4, layers)),
        dma((4, layers)),
        dma((2,)),
        dma((na,)),
        dma((na,)),
        dma((nb,)),
        dma((nb,)),
        dma((2,)),
        dma((2,)),
    ]
    in_vmem = pl.BlockSpec(memory_space=pltpu.VMEM)
    anywhere = pl.BlockSpec(memory_space=pl.ANY)
    rec, eg, bg, dg = pl.pallas_call(
        functools.partial(kernel, sizes),
        out_shape=(
            jax.ShapeDtypeStruct((rows, width), BF),
            jax.ShapeDtypeStruct((layers, dl, lats), BF),
            jax.ShapeDtypeStruct((layers, lats), F32),
            jax.ShapeDtypeStruct((pairs, dl, lats), BF),
        ),
        in_specs=[in_vmem, in_vmem, anywhere, in_vmem, anywhere, in_vmem],
        out_specs=(in_vmem,) * 4,
        scratch_shapes=scratch,
        compiler_params=pltpu.CompilerParams(
            collective_id=0, has_side_effects=True, vmem_limit_bytes=48 * 1024 * 1024
        ),
    )(layer_inputs, layer_outputs.reshape(rows, width), encoder, encoder_bias, decoder, active_blocks)
    return rec.reshape(rows, layers, dl), eg, bg, dg


def solution(mesh):
    ny, nl = mesh.shape["layer"] // 4, mesh.shape["lat"]

    def local(layer_inputs, layer_outputs, encoder, encoder_bias, decoder, active_blocks):
        layers, dl, lats = encoder.shape
        rows = layer_outputs.shape[0]
        chunk = -(-2 * rows // 16) * 16
        sizes = (layers, dl, lats, rows, ny, nl, chunk)
        return step(sizes, layer_inputs, layer_outputs, encoder, encoder_bias, decoder, active_blocks)

    return jax.shard_map(
        local,
        mesh=mesh,
        in_specs=(
            P(None, "lat", "layer"),
            P("layer", None, "lat"),
            P(None, "lat", "layer"),
            P(None, "layer"),
            P(None, "lat", "layer"),
            P(),
        ),
        out_specs=(
            P("layer", None, "lat"),
            P(None, "lat", "layer"),
            P(None, "layer"),
            P(None, "lat", "layer"),
        ),
        check_vma=False,
    )
```

time: 819 us -> 120 us (0.15)
  the two profiles are of different devices: /device:TPU:1 before, /device:TPU:5 now
where the time goes in v1:
time: 120 us
  Pallas kernels  110 us (92%)
  local copies, waits for them, and re-layouts  8.75 us (7%)
    pallas_call x1, Pallas kernels, step(): pl.pallas_call(functools.partial(kernel, sizes), out_shape=(jax.ShapeDtyp...  110 us
    unnamed x11, local copies, waits for them, and re-layouts  7.12 us

profile of v1, /device:TPU:5, one launch (start us, length us, event | category | flops | bytes accessed | tf_op | source)
XLA Modules:
  0.0 119.6 jit_solution(2876877798504108902)
XLA Ops:
  0.6 1.0 copy.10.x_ref
  1.6 0.8 copy.11.act_ref
  2.4 0.9 reshape.14.y_ref
  3.3 0.0 copy-start
  3.4 1.2 %copy-done = bf16[10,224,256]{2,1,0:T(8,128)(2,1)S(1)} copy-done((bf16[10,224,256]{2,1,0:T(8,128)(2,1)S(1)}, bf16[10,224,256]{2,1,0:T(8,128)(2,1)}, u32[]{:S(2)}) %copy-start) | copy-done | bytes 1146904
  4.6 0.0 copy-start.1
  4.6 1.0 copy-done.1
  5.6 0.0 copy-start.2
  5.6 0.7 copy-done.2
  6.3 110.1 %shard_map.93 = (bf16[22,896]{1,0:T(8,128)(2,1)S(1)}, bf16[4,224,256]{2,1,0:T(8,128)(2,1)S(1)}, f32[4,256]{1,0:T(4,128)S(1)}, bf16[10,224,256]{2,1,0:T(8,128)(2,1)S(1)}) custom-call(bf16[4,224,22]{2,1,0:T(8,128)(2,1)S(1)} %copy.10.x_ref, bf16[22,896]{1,0:T(8,128)(2,1)S(1)} %reshape.14.y_ref, bf16[4,224,256]{2,1,0:T(8,128)(2,1)S(1)} %copy-done.1, ...), custom_call_target="tpu_custom_call" | custom-call | tf_op jit(solution)/shard_map/pallas_call | solution.py:488
  116.5 0.7 reshape.15
  117.2 0.8 copy.15
  118.0 0.6 copy.16
  118.6 1.0 copy.17
Async XLA Ops:
  3.3 1.3 %copy-start = (bf16[10,224,256]{2,1,0:T(8,128)(2,1)S(1)}, bf16[10,224,256]{2,1,0:T(8,128)(2,1)}, u32[]{:S(2)}) copy-start(bf16[10,224,256]{2,1,0:T(8,128)(2,1)} %dec_ref.1) | copy-start | bytes 3440644
  4.6 1.0 copy-start.1
  5.6 0.7 copy-start.2

commit v2 on v1

--- a/solution.py
+++ b/solution.py
@@ -29,8 +29,8 @@
     rec_ref, eg_ref, bg_ref, dg_ref,
     xg, eg, xt, et, cd, pgd, encp, dcat, sel, selt,
     xy_s, xy_r, pk, rx, ck, pc, rc, pg, slope,
-    hm_s, hm_r, ho, ra_s, ra_r, rb_s, rb_r, fx_s, fx_r, recb,
-    load_sem, xy_sem, ag_x, ag_as, ag_ar, ag_bs, ag_br, ag_ms, ag_mr,
+    hm_s, hm_r, ho, ra_s, ra_r, rb_s, rb_r, fx_s, fx_r, recb, yc, x_in, y_in, act_in, bias_in,
+    load_sem, xy_out, xy_sem, ag_as, ag_ar, ag_bs, ag_br, ag_ms, ag_mr,
     lat_s, lat_r, hm_sem, rs_as, rs_ar, rs_bs, rs_br, fx_sem, rec_sem,
 ):
     layers, dl, lats, rows, ny, nl, chunk = sizes
@@ -63,8 +63,10 @@
     def local(offset):
         return place(0, offset)
 
+    diagonal = at(1 - h, y, 1 - core)
+
     barrier = pltpu.get_barrier_semaphore()
-    for peer in (mate, partner, to_a, to_b):
+    for peer in (mate, partner, diagonal, to_a, to_b):
         pl.semaphore_signal(barrier, inc=1, device_id=peer)
 
     def greet(d, carry):
@@ -72,112 +74,159 @@
         return carry
 
     lax.fori_loop(1, nl, greet, 0)
-    pl.semaphore_wait(barrier, 4 + nl - 1)
-
-    put = jnp.where(iota((chunk, rows), 0) == iota((chunk, rows), 1) + rows * core, 1.0, 0.0).astype(BF)
-    xy_s[0:chunk, :] = dot(put, x_ref[...].reshape(width, rows), ((1,), (1,))).astype(BF)
-    xy_s[chunk : 2 * chunk, :] = dot(put, y_ref[...]).astype(BF)
-    xy_copy = pltpu.make_async_remote_copy(xy_s, xy_r, xy_sem.at[0], xy_sem.at[1], device_id=mate)
-    xy_copy.start()
-
+
+    loads = [
+        pltpu.make_async_copy(x_ref, x_in, load_sem.at[0]),
+        pltpu.make_async_copy(y_ref, y_in, load_sem.at[1]),
+        pltpu.make_async_copy(act_ref, act_in, load_sem.at[2]),
+        pltpu.make_async_copy(bias_ref, bias_in, load_sem.at[3]),
+    ]
+    for copy in loads:
+        copy.start()
     encp[...] = jnp.zeros_like(encp)
     dcat[...] = jnp.zeros_like(dcat)
-    loads = []
 
     def first(s):
         return min(dl * s // LANE * LANE, width - span)
 
+    enc_loads, dec_loads = [], []
     for s in range(layers):
-        loads.append(pltpu.make_async_copy(enc_ref.at[s], encp.at[s, pl.ds(dl * s - first(s), dl)], load_sem.at[s]))
+        where = encp.at[s, pl.ds(dl * s - first(s), dl)]
+        enc_loads.append(pltpu.make_async_copy(enc_ref.at[s], where, load_sem.at[4 + s]))
     for t in range(layers):
         for s in range(t + 1):
             pair = t * (t + 1) // 2 + s
-            loads.append(
-                pltpu.make_async_copy(
-                    dec_ref.at[pair], dcat.at[pl.ds(dl * t, dl), pl.ds(lats * s, lats)], load_sem.at[layers + pair]
-                )
-            )
-    for copy in loads:
+            where = dcat.at[pl.ds(dl * t, dl), pl.ds(lats * s, lats)]
+            dec_loads.append(pltpu.make_async_copy(dec_ref.at[pair], where, load_sem.at[4 + layers + pair]))
+    for copy in enc_loads + dec_loads:
         copy.start()
 
-    xy_copy.wait_recv()
-    xg_own = place(core, 0)
+    def flat(ref):
+        return jnp.concatenate([ref[:, s, :] for s in range(layers)], axis=1)
+
+    pad = jnp.zeros((32 - rows, width), BF)
+    loads[0].wait()
+    xy_s[0] = jnp.concatenate([flat(x_in), pad], axis=0)
+    loads[1].wait()
+    xy_s[1] = jnp.concatenate([flat(y_in), pad], axis=0)
+
+    pl.semaphore_wait(barrier, 5 + nl - 1)
+
+    def xy_copy(n, to, w):
+        return pltpu.make_async_remote_copy(
+            xy_s.at[n], xy_r.at[n, w], xy_out.at[n, w], xy_sem.at[n, w], device_id=to
+        )
+
+    for n in range(2):
+        @pl.when(owner)
+        def _():
+            xy_copy(n, partner, core).start()
+
+        @pl.when(jnp.logical_not(owner))
+        def _():
+            xy_copy(n, mate, core).start()
+            pltpu.make_async_remote_copy(
+                xy_s.at[n], xy_r.at[n, core], xy_out.at[n, 1 - core], xy_sem.at[n, core], device_id=diagonal
+            ).start()
+
+    def merged(n):
+        total = None
+        for w in range(2):
+            there, here = iota((chunk, 32), 0), iota((chunk, 32), 1)
+            put = jnp.where((there == here + rows * w) & (here < rows), 1.0, 0.0).astype(BF)
+            part = dot(put, xy_r[n, w])
+            total = part if total is None else total + part
+        return total.astype(BF)
+
+    def xy_arrive(n):
+        @pl.when(owner)
+        def _():
+            xy_r[n, core] = xy_s[n]
+            xy_copy(n, mate, 1 - core).wait_recv()
+
+        @pl.when(jnp.logical_not(owner))
+        def _():
+            for w in range(2):
+                xy_copy(n, mate, w).wait_recv()
+
+        return merged(n)
+
+    cuts = [(0, 3 * LANE), (3 * LANE, 5 * LANE), (5 * LANE, width)]
+    nc = len(cuts)
 
     def gather_copies(buf, n):
-        def ring(to, offset, send, recv):
-            where = buf.at[place(core, offset)]
+        def ring(to, offset, send, recv, lanes):
+            where = buf.at[place(core, offset), pl.ds(lanes[0], lanes[1] - lanes[0])]
             return pltpu.make_async_remote_copy(where, where, send, recv, device_id=to)
 
-        cross = ring(partner, 0, ag_x.at[n, 0], ag_x.at[n, 1])
-        a_out = [ring(to_a, -i, ag_as.at[n, i], ag_ar.at[n, i]) for i in range(na)]
-        b_out = [ring(to_b, i, ag_bs.at[n, i], ag_br.at[n, i]) for i in range(nb)]
-        a_in = [ring(to_a, -i - 1, ag_as.at[n, i], ag_ar.at[n, i]) for i in range(na)]
-        b_in = [ring(to_b, i + 1, ag_bs.at[n, i], ag_br.at[n, i]) for i in range(nb)]
+        def rings(to, sign, shift, count, send, recv):
+            return [
+                [ring(to, sign * (i + shift), send.at[n, i, c], recv.at[n, i, c], cuts[c]) for c in range(nc)]
+                for i in range(count)
+            ]
+
+        a_out, a_in = rings(to_a, -1, 0, na, ag_as, ag_ar), rings(to_a, -1, 1, na, ag_as, ag_ar)
+        b_out, b_in = rings(to_b, 1, 0, nb, ag_bs, ag_br), rings(to_b, 1, 1, nb, ag_bs, ag_br)
         order = [0]
         for i in range(na):
             order.append(-i - 1)
             if i < nb:
                 order.append(i + 1)
-        pass_on = [ring(mate, o, ag_ms.at[n, j], ag_mr.at[n, j]) for j, o in enumerate(order)]
-        from_mate = []
+        pass_on, from_mate = [], []
         for j, o in enumerate(order):
+            where = buf.at[place(core, o)]
+            pass_on.append(
+                pltpu.make_async_remote_copy(where, where, ag_ms.at[n, j], ag_mr.at[n, j], device_id=mate)
+            )
             where = buf.at[place(1 - core, -o)]
-            from_mate.append(pltpu.make_async_remote_copy(where, where, ag_ms.at[n, j], ag_mr.at[n, j], device_id=mate))
-        return cross, a_out, b_out, a_in, b_in, pass_on, from_mate
-
-    def gather_start(copies):
-        cross, a_out, b_out, a_in, b_in, pass_on, from_mate = copies
-
-        @pl.when(owner)
-        def _():
-            cross.start()
-
-        @pl.when(jnp.logical_not(owner))
-        def _():
-            cross.wait_recv()
-
-        a_out[0].start()
+            from_mate.append(
+                pltpu.make_async_remote_copy(where, where, ag_ms.at[n, j], ag_mr.at[n, j], device_id=mate)
+            )
+        return a_out, b_out, a_in, b_in, pass_on, from_mate
+
+    def gather_start(copies, c):
+        copies[0][0][c].start()
         if nb:
-            b_out[0].start()
+            copies[1][0][c].start()
+
+    def gather_run(copies, extra):
+        a_out, b_out, a_in, b_in, pass_on, from_mate = copies
         pass_on[0].start()
-
-    def gather_run(copies):
-        cross, a_out, b_out, a_in, b_in, pass_on, from_mate = copies
         j = 1
         for i in range(na):
-            a_in[i].wait_recv()
-            if i + 1 < na:
-                a_out[i + 1].start()
-            pass_on[j].start()
-            j += 1
-            if i < nb:
-                b_in[i].wait_recv()
-                if i + 1 < nb:
-                    b_out[i + 1].start()
+            for c in range(nc):
+                a_in[i][c].wait_recv()
+                if i + 1 < na:
+                    a_out[i + 1][c].start()
+                if i < nb:
+                    b_in[i][c].wait_recv()
+                    if i + 1 < nb:
+                        b_out[i + 1][c].start()
+            for _ in range(2 if i < nb else 1):
                 pass_on[j].start()
                 j += 1
+            if i < len(extra):
+                extra[i]()
+        for more in extra[na:]:
+            more()
         for copy in from_mate:
             copy.wait_recv()
 
     def gather_end(copies):
-        cross, a_out, b_out, a_in, b_in, pass_on, from_mate = copies
-
-        @pl.when(owner)
-        def _():
-            cross.wait_send()
-
-        for copy in a_out + b_out + pass_on:
+        a_out, b_out, a_in, b_in, pass_on, from_mate = copies
+        for group in a_out + b_out:
+            for copy in group:
+                copy.wait_send()
+        for copy in pass_on:
             copy.wait_send()
 
+    own = place(core, 0)
     x_copies = gather_copies(xg, 0)
-
-    @pl.when(owner)
-    def _():
-        xg[xg_own, :] = xy_s[0:chunk, :] + xy_r[0:chunk, :]
-
-    gather_start(x_copies)
-
-    nr = act_ref.shape[1]
+    xg[own, :] = xy_arrive(0)
+    for c in range(nc):
+        gather_start(x_copies, c)
+
+    nr = act_in.shape[2]
     ii, jj = iota((nr, nr), 0), iota((nr, nr), 1)
     lane_place = iota((1, places), 1)
     lane_chip = jnp.zeros((1, places), jnp.int32)
@@ -192,31 +241,34 @@
     row_rank = (m1 // ROWBLOCK).astype(F32)
     row_value = (ROWBLOCK * r0 + m1 % ROWBLOCK + 1).astype(F32)
     chip_in = iota((chunk, SLOTS), 0)
-
-    def choose(s, carry):
-        named = act_ref[s]
+    chip_row = jnp.where(chip_in < real, chip_in, -places).astype(F32)
+    loads[2].wait()
+    loads[3].wait()
+
+    def choose(s):
+        named = act_in[s]
         for b in range(2):
-            hit = jnp.max(jnp.where(named == 2 * me + b, 1.0, 0.0), axis=1, keepdims=True)
-            across = jnp.broadcast_to(hit, (nr, nr))
-            hit_row = jnp.sum(jnp.where(ii == jj, across, 0.0), axis=0, keepdims=True)
-            rank_row = jnp.sum(jnp.where(ii < jj, across, 0.0), axis=0, keepdims=True)
-            rank = jnp.sum(jnp.where(jj < ii, jnp.broadcast_to(hit_row, (nr, nr)), 0.0), axis=1, keepdims=True)
+            hit_row = jnp.max(jnp.where(named == 2 * me + b, 1.0, 0.0), axis=0, keepdims=True)
+            across = jnp.broadcast_to(hit_row, (nr, nr))
+            hit = jnp.sum(jnp.where(ii == jj, across, 0.0), axis=1, keepdims=True)
+            rank = jnp.sum(jnp.where(jj < ii, across, 0.0), axis=1, keepdims=True)
+            rank_row = jnp.sum(jnp.where(ii < jj, jnp.broadcast_to(hit, (nr, nr)), 0.0), axis=0, keepdims=True)
             rank_row = jnp.where(hit_row > 0, rank_row, -1.0)
             rank = jnp.where(hit > 0, rank, -1.0)
             want = jnp.sum(jnp.where(rank_row == col_rank, col_value, 0.0), axis=1, keepdims=True) - 1.0
             want_row = jnp.sum(jnp.where(rank == row_rank, row_value, 0.0), axis=0, keepdims=True) - 1.0
             sel[s, b * SLOTS : (b + 1) * SLOTS, :] = jnp.where(want == lane_row, 1.0, 0.0).astype(BF)
             for c in range(2 * ny):
-                row = jnp.where(chip_in < real, chip_in + c * real, -2).astype(F32)
                 selt[s, c * chunk : (c + 1) * chunk, b * SLOTS : (b + 1) * SLOTS] = jnp.where(
-                    row == want_row, 1.0, 0.0
+                    chip_row == want_row - float(c * real), 1.0, 0.0
                 ).astype(BF)
-        return carry
-
-    lax.fori_loop(0, layers, choose, 0)
-
-    gather_run(x_copies)
-    for copy in loads[:layers]:
+
+    def outputs():
+        yc[...] = xy_arrive(1)
+
+    choose(0)
+    gather_run(x_copies, [functools.partial(choose, s) for s in range(1, layers)] + [outputs])
+    for copy in enc_loads:
         copy.wait()
 
     def lat_rows(j):
@@ -266,7 +318,7 @@
     for s in range(layers):
         lat_wait(lat_r, s, 0)
         total = jnp.sum(rx[s].astype(F32), axis=0)
-        bias = jnp.where(b_of == 0, bias_ref[s : s + 1, 0:BLOCK], bias_ref[s : s + 1, BLOCK : 2 * BLOCK])
+        bias = jnp.where(b_of == 0, bias_in[s : s + 1, 0:BLOCK], bias_in[s : s + 1, BLOCK : 2 * BLOCK])
         pre = total + bias
         small = jnp.exp(-jnp.abs(pre))
         ck[s, lat_rows(q), :] = (jnp.maximum(pre, 0.0) + jnp.log1p(small)).astype(BF)
@@ -288,7 +340,7 @@
         lat_wait(lat_r, s, 1)
         unpack(ck, cd, s)
 
-    for copy in loads[layers:]:
+    for copy in dec_loads:
         copy.wait()
 
     tiles = [min(layers, ((n + 1) * LANE - 1) // dl + 1) for n in range(width // LANE)]
@@ -299,73 +351,95 @@
         else:
             groups.append([n, n + 1, count])
 
-    def decode(hh, out):
+    def decode(hh, out, c):
         base = pl.ds(pl.multiple_of(hh * half, 16), half)
         for lo, hi, count in groups:
-            lanes = slice(lo * LANE, hi * LANE)
-            out[:, lanes] = dot(cd[base, 0 : count * lats], dcat[lanes, 0 : count * lats], ((1,), (1,))).astype(out.dtype)
-
-    decode(1 - core, hm_s)
-    hm_copy = pltpu.make_async_remote_copy(hm_s, hm_r, hm_sem.at[0], hm_sem.at[1], device_id=mate)
-    hm_copy.start()
-    decode(core, ho)
-    hm_copy.wait_recv()
-
-    def mine(offset):
-        return ho[local(offset), :] + hm_r[local(offset), :].astype(F32)
-
-    a_copies = [
-        pltpu.make_async_remote_copy(ra_s.at[i], ra_r.at[i], rs_as.at[i], rs_ar.at[i], device_id=to_a) for i in range(na)
-    ]
-    b_copies = [
-        pltpu.make_async_remote_copy(rb_s.at[i], rb_r.at[i], rs_bs.at[i], rs_br.at[i], device_id=to_b) for i in range(nb)
-    ]
+            if cuts[c][0] <= lo * LANE < cuts[c][1]:
+                lanes = slice(lo * LANE, hi * LANE)
+                part = dot(cd[base, 0 : count * lats], dcat[lanes, 0 : count * lats], ((1,), (1,)))
+                out[:, lanes] = part.astype(out.dtype)
+
+    def lanes_of(c):
+        return pl.ds(cuts[c][0], cuts[c][1] - cuts[c][0])
+
+    hm_copies = []
+    for c in range(nc):
+        decode(1 - core, hm_s, c)
+        hm_copies.append(
+            pltpu.make_async_remote_copy(
+                hm_s.at[:, lanes_of(c)], hm_r.at[:, lanes_of(c)], hm_sem.at[0, c], hm_sem.at[1, c], device_id=mate
+            )
+        )
+        hm_copies[c].start()
+
+    def mine(offset, c):
+        return ho[local(offset), lanes_of(c)] + hm_r[local(offset), lanes_of(c)].astype(F32)
+
+    def sums(to, count, buf_s, buf_r, send, recv):
+        return [
+            [
+                pltpu.make_async_remote_copy(
+                    buf_s.at[i, :, lanes_of(c)], buf_r.at[i, :, lanes_of(c)], send.at[i, c], recv.at[i, c], device_id=to
+                )
+                for c in range(nc)
+            ]
+            for i in range(count)
+        ]
+
+    a_copies = sums(to_a, na, ra_s, ra_r, rs_as, rs_ar)
+    b_copies = sums(to_b, nb, rb_s, rb_r, rs_bs, rs_br)
+
+    def forward(copies, buf_s, buf_r, i, offset, c):
+        part = mine(offset, c)
+        if i:
+            copies[i - 1][c].wait_recv()
+            part = part + buf_r[i - 1, :, lanes_of(c)].astype(F32)
+        buf_s[i, :, lanes_of(c)] = part.astype(BF)
+        copies[i][c].start()
+
     for i in range(na):
-        part = mine(na - i)
-        if i:
-            a_copies[i - 1].wait_recv()
-            part = part + ra_r[i - 1].astype(F32)
-        ra_s[i] = part.astype(BF)
-        a_copies[i].start()
-        if i < nb:
-            part = mine(i - nb)
-            if i:
-                b_copies[i - 1].wait_recv()
-                part = part + rb_r[i - 1].astype(F32)
-            rb_s[i] = part.astype(BF)
-            b_copies[i].start()
-    total = mine(0)
-    a_copies[na - 1].wait_recv()
-    total = total + ra_r[na - 1].astype(F32)
-    if nb:
-        b_copies[nb - 1].wait_recv()
-        total = total + rb_r[nb - 1].astype(F32)
-    ho[local(0), :] = total
-
-    fx_copy = pltpu.make_async_remote_copy(fx_s, fx_r, fx_sem.at[0], fx_sem.at[1], device_id=partner)
+        for c in range(nc):
+            if i == 0:
+                decode(core, ho, c)
+                hm_copies[c].wait_recv()
+            forward(a_copies, ra_s, ra_r, i, na - i, c)
+            if i < nb:
+                forward(b_copies, rb_s, rb_r, i, i - nb, c)
+    fx_copies = []
+    for c in range(nc):
+        total = mine(0, c)
+        a_copies[na - 1][c].wait_recv()
+        total = total + ra_r[na - 1, :, lanes_of(c)].astype(F32)
+        if nb:
+            b_copies[nb - 1][c].wait_recv()
+            total = total + rb_r[nb - 1, :, lanes_of(c)].astype(F32)
+        fx_s[:, lanes_of(c)] = total.astype(BF)
+        fx_copies.append(
+            pltpu.make_async_remote_copy(
+                fx_s.at[:, lanes_of(c)], fx_r.at[:, lanes_of(c)], fx_sem.at[0, c], fx_sem.at[1, c], device_id=partner
+            )
+        )
+        fx_copies[c].start()
+
+    e_copies = gather_copies(eg, 1)
+    for c in range(nc):
+        fx_copies[c].wait_recv()
+        lanes = lanes_of(c)
+        whole = fx_s[:, lanes].astype(F32) + fx_r[:, lanes].astype(F32)
+        eg[own, lanes] = (whole - yc[:, lanes].astype(F32)).astype(BF)
+        gather_start(e_copies, c)
+
+        @pl.when(owner)
+        def _():
+            recb[:, lanes] = whole.astype(BF)
+
     rec_copy = pltpu.make_async_remote_copy(recb, recb, rec_sem.at[0], rec_sem.at[1], device_id=mate)
-    e_copies = gather_copies(eg, 1)
-
-    @pl.when(jnp.logical_not(owner))
-    def _():
-        fx_s[...] = ho[local(0), :].astype(BF)
-        fx_copy.start()
-
-    @pl.when(owner)
-    def _():
-        fx_copy.wait_recv()
-        whole = ho[local(0), :] + fx_r[...].astype(F32)
-        outs = xy_s[chunk : 2 * chunk, :].astype(F32) + xy_r[chunk : 2 * chunk, :].astype(F32)
-        eg[xg_own, :] = (whole - outs).astype(BF)
-        recb[...] = whole.astype(BF)
-
-    gather_start(e_copies)
 
     @pl.when(owner)
     def _():
         rec_copy.start()
 
-    gather_run(e_copies)
+    gather_run(e_copies, [])
 
     for s in range(layers - 1, -1, -1):
         low = dl * s // LANE * LANE
@@ -408,16 +482,23 @@
 
     @pl.when(jnp.logical_not(owner))
     def _():
-        fx_copy.wait_send()
         rec_copy.wait_recv()
 
     take = jnp.where(iota((rows, chunk), 1) == iota((rows, chunk), 0) + rows * core, 1.0, 0.0).astype(BF)
     rec_ref[...] = dot(take, recb[...]).astype(BF)
 
-    xy_copy.wait_send()
-    hm_copy.wait_send()
-    for copy in a_copies + b_copies:
+    for n in range(2):
+        xy_copy(n, mate, core).wait_send()
+
+        @pl.when(jnp.logical_not(owner))
+        def _():
+            xy_copy(n, mate, 1 - core).wait_send()
+
+    for copy in hm_copies + fx_copies:
         copy.wait_send()
+    for group in a_copies + b_copies:
+        for copy in group:
+            copy.wait_send()
     gather_end(x_copies)
     gather_end(e_copies)
     for n in range(4):
@@ -445,8 +526,8 @@
         vmem((width, layers * lats), BF),
         vmem((layers, 2 * SLOTS, places), BF),
         vmem((layers, places, 2 * SLOTS), BF),
-        vmem((2 * chunk, width), BF),
-        vmem((2 * chunk, width), BF),
+        vmem((2, 32, width), BF),
+        vmem((2, 2, 32, width), BF),
         vmem((layers, 2 * SLOTS, BLOCK), BF),
         vmem((layers, nl, shard, BLOCK), BF),
         vmem((layers, 2 * SLOTS, BLOCK), BF),
@@ -464,23 +545,28 @@
         vmem(ring, BF),
         vmem(ring, BF),
         vmem(ring, BF),
-        dma((layers + pairs,)),
-        dma((2,)),
+        vmem(ring, BF),
+        vmem((rows, layers, dl), BF),
+        vmem((rows, layers, dl), BF),
+        vmem((layers, active_blocks.shape[2], active_blocks.shape[1]), jnp.int32),
+        vmem((layers, lats), F32),
+        dma((4 + layers + pairs,)),
         dma((2, 2)),
-        dma((2, na)),
-        dma((2, na)),
-        dma((2, nb)),
-        dma((2, nb)),
+        dma((2, 2)),
+        dma((2, na, 3)),
+        dma((2, na, 3)),
+        dma((2, nb, 3)),
+        dma((2, nb, 3)),
         dma((2, ny)),
         dma((2, ny)),
         dma((4, layers)),
         dma((4, layers)),
-        dma((2,)),
-        dma((na,)),
-        dma((na,)),
-        dma((nb,)),
-        dma((nb,)),
-        dma((2,)),
+        dma((2, 3)),
+        dma((na, 3)),
+        dma((na, 3)),
+        dma((nb, 3)),
+        dma((nb, 3)),
+        dma((2, 3)),
         dma((2,)),
     ]
     in_vmem = pl.BlockSpec(memory_space=pltpu.VMEM)
@@ -493,13 +579,20 @@
             jax.ShapeDtypeStruct((layers, lats), F32),
             jax.ShapeDtypeStruct((pairs, dl, lats), BF),
         ),
-        in_specs=[in_vmem, in_vmem, anywhere, in_vmem, anywhere, in_vmem],
+        in_specs=[anywhere] * 6,
         out_specs=(in_vmem,) * 4,
         scratch_shapes=scratch,
         compiler_params=pltpu.CompilerParams(
-            collective_id=0, has_side_effects=True, vmem_limit_bytes=48 * 1024 * 1024
+            collective_id=0, has_side_effects=True, vmem_limit_bytes=60 * 1024 * 1024
         ),
-    )(layer_inputs, layer_outputs.reshape(rows, width), encoder, encoder_bias, decoder, active_blocks)
+    )(
+        layer_inputs.transpose(2, 0, 1),
+        layer_outputs,
+        encoder,
+        encoder_bias,
+        decoder,
+        active_blocks.transpose(0, 2, 1),
+    )
     return rec.reshape(rows, layers, dl), eg, bg, dg
 
 

time: 120 us -> 112 us (0.933)
  the two profiles are of different devices: /device:TPU:5 before, /device:TPU:1 now
where the time goes in v2:
time: 112 us
  Pallas kernels  104 us (93%)
  local copies, waits for them, and re-layouts  6.93 us (6%)
    pallas_call x1, Pallas kernels, step(): pl.pallas_call(functools.partial(kernel, sizes), out_shape=(jax.ShapeDtyp...  104 us
    unnamed x3, local copies, waits for them, and re-layouts  5.42 us

profile of v2, /device:TPU:1, one launch (start us, length us, event | category | flops | bytes accessed | tf_op | source)
XLA Modules:
  0.0 111.8 jit_solution(9764030412005354049)
XLA Ops:
  0.6 104.2 %shard_map.93 = (bf16[22,896]{1,0:T(8,128)(2,1)}, bf16[4,224,256]{2,1,0:T(8,128)(2,1)}, f32[4,256]{1,0:T(4,128)}, bf16[10,224,256]{2,1,0:T(8,128)(2,1)}) custom-call(bf16[22,4,224]{2,1,0:T(4,128)(2,1)} %bitcast.2, bf16[22,4,224]{2,1,0:T(4,128)(2,1)} %y_ref.1, bf16[4,224,256]{2,1,0:T(8,128)(2,1)} %enc_ref.1, f32[4,256]{1,0:T(4,128)} %bias_ref.1, ...), custom_call_target="tpu_custom_call" | custom-call | tf_op jit(solution)/shard_map/pallas_call | solution.py:574
  104.8 1.5 %reshape.11 = bf16[22,4,224]{2,1,0:T(4,128)(2,1)} reshape(bf16[22,896]{1,0:T(8,128)(2,1)} %get-tuple-element.8) | data formatting | bytes 78848 | tf_op jit(solution)/shard_map/reshape | solution.py:596
  106.3 1.8 %copy.13 = bf16[4,224,256]{2,1,0:T(8,128)(2,1)} copy(bf16[4,224,256]{2,1,0:T(8,128)(2,1)} %get-tuple-element.17) | data formatting | bytes 917504
  108.1 1.3 %copy.14 = f32[4,256]{1,0:T(4,128)} copy(f32[4,256]{1,0:T(4,128)} %get-tuple-element.18) | data formatting | bytes 8192
  109.4 2.3 %copy.15 = bf16[10,224,256]{2,1,0:T(8,128)(2,1)} copy(bf16[10,224,256]{2,1,0:T(8,128)(2,1)} %get-tuple-element.19) | data formatting | bytes 2293760

commit v3 on v2

--- a/solution.py
+++ b/solution.py
@@ -28,10 +28,10 @@
     x_ref, y_ref, enc_ref, bias_ref, dec_ref, act_ref,
     rec_ref, eg_ref, bg_ref, dg_ref,
     xg, eg, xt, et, cd, pgd, encp, dcat, sel, selt,
-    xy_s, xy_r, pk, rx, ck, pc, rc, pg, slope,
+    xy_s, xy_r, xs, xr, keep, zs, zr, cz, slope,
     hm_s, hm_r, ho, ra_s, ra_r, rb_s, rb_r, fx_s, fx_r, recb, yc, x_in, y_in, act_in, bias_in,
     load_sem, xy_out, xy_sem, ag_as, ag_ar, ag_bs, ag_br, ag_ms, ag_mr,
-    lat_s, lat_r, hm_sem, rs_as, rs_ar, rs_bs, rs_br, fx_sem, rec_sem,
+    x_out, x_arr, z_out, z_arr, c_out, c_arr, cx_out, cx_arr, hm_sem, rs_as, rs_ar, rs_bs, rs_br, fx_sem, rec_sem,
 ):
     layers, dl, lats, rows, ny, nl, chunk = sizes
     width = layers * dl
@@ -39,7 +39,8 @@
     half = ny * chunk
     places = 2 * half
     real = 2 * rows
-    shard = 2 * SLOTS // nl
+    nz = nl // 2
+    shard = SLOTS // nz
     na, nb = ny // 2, ny // 2 - 1
 
     me, q = lax.axis_index("layer"), lax.axis_index("lat")
@@ -64,16 +65,21 @@
         return place(0, offset)
 
     diagonal = at(1 - h, y, 1 - core)
+    x_lo, z = q // nz, lax.rem(q, nz)
+    beside = {"layer": me, "lat": (1 - x_lo) * nz + z}
+
+    def along(d):
+        return {"layer": me, "lat": x_lo * nz + lax.rem(z + d, nz)}
 
     barrier = pltpu.get_barrier_semaphore()
-    for peer in (mate, partner, diagonal, to_a, to_b):
+    for peer in (mate, partner, diagonal, to_a, to_b, beside):
         pl.semaphore_signal(barrier, inc=1, device_id=peer)
 
     def greet(d, carry):
-        pl.semaphore_signal(barrier, inc=1, device_id={"layer": me, "lat": lax.rem(q + d, nl)})
+        pl.semaphore_signal(barrier, inc=1, device_id=along(d))
         return carry
 
-    lax.fori_loop(1, nl, greet, 0)
+    lax.fori_loop(1, nz, greet, 0)
 
     loads = [
         pltpu.make_async_copy(x_ref, x_in, load_sem.at[0]),
@@ -110,7 +116,7 @@
     loads[1].wait()
     xy_s[1] = jnp.concatenate([flat(y_in), pad], axis=0)
 
-    pl.semaphore_wait(barrier, 5 + nl - 1)
+    pl.semaphore_wait(barrier, 6 + nz - 1)
 
     def xy_copy(n, to, w):
         return pltpu.make_async_remote_copy(
@@ -271,77 +277,95 @@
     for copy in enc_loads:
         copy.wait()
 
-    def lat_rows(j):
-        return pl.ds(pl.multiple_of(j * shard, 16), shard)
-
-    def scatter(src, dst, s, n):
+    def x_copy(n, s):
+        return pltpu.make_async_remote_copy(
+            xs.at[n, s], xr.at[n, s], x_out.at[n, s], x_arr.at[n, s], device_id=beside
+        )
+
+    def pack(dense, n, s):
+        both = dot(sel[s], dense)
+        low, high = both[0:SLOTS, 0:BLOCK], both[SLOTS : 2 * SLOTS, BLOCK : 2 * BLOCK]
+        keep[n, s] = jnp.where(x_lo == 0, low, high)
+        xs[n, s] = jnp.where(x_lo == 0, high, low).astype(BF)
+        x_copy(n, s).start()
+
+    def z_copy(n, g, d):
+        peer = lax.rem(z + d, nz)
+        return pltpu.make_async_remote_copy(
+            zs.at[n, g, peer], zr.at[n, g, z], z_out.at[n, g], z_arr.at[n, g], device_id=along(d)
+        )
+
+    def c_copy(n, g, d):
+        where = cz.at[n, g, x_lo, z]
+        return pltpu.make_async_remote_copy(where, where, c_out.at[n, g], c_arr.at[n, g], device_id=along(d))
+
+    def cx_copy(n, g, half_of):
+        where = cz.at[n, g, half_of]
+        return pltpu.make_async_remote_copy(where, where, cx_out.at[n, g], cx_arr.at[n, g], device_id=beside)
+
+    def all_along(copy, n, g):
         def one(d, carry):
-            peer = lax.rem(q + d, nl)
-            pltpu.make_async_remote_copy(
-                src.at[s, lat_rows(peer)], dst.at[s, q], lat_s.at[n, s], lat_r.at[n, s],
-                device_id={"layer": me, "lat": peer},
-            ).start()
+            copy(n, g, d).start()
             return carry
 
-        lax.fori_loop(1, nl, one, 0)
-        dst[s, q] = src[s, lat_rows(q), :]
-
-    def spread(buf, s, n):
-        def one(d, carry):
-            where = buf.at[s, lat_rows(q)]
-            pltpu.make_async_remote_copy(
-                where, where, lat_s.at[n, s], lat_r.at[n, s], device_id={"layer": me, "lat": lax.rem(q + d, nl)}
-            ).start()
-            return carry
-
-        lax.fori_loop(1, nl, one, 0)
-
-    def lat_wait(sem, s, n):
-        where = ck.at[s, pl.ds(0, (nl - 1) * shard)]
-        pltpu.make_async_copy(where, where, sem.at[n, s]).wait()
-
-    def pack(dense, dst, s):
-        both = dot(sel[s], dense)
-        for b in range(2):
-            part = slice(b * SLOTS, (b + 1) * SLOTS)
-            dst[s, part, :] = both[part, b * BLOCK : (b + 1) * BLOCK].astype(BF)
+        lax.fori_loop(1, nz, one, 0)
+
+    def wait_along(sem, n, g):
+        where = zr.at[n, g, pl.ds(0, nz - 1)]
+        pltpu.make_async_copy(where, where, sem.at[n, g]).wait()
+
+    def z_send(n, g, members):
+        for i, s in enumerate(members):
+            x_copy(n, s).wait_recv()
+            total = keep[n, s] + xr[n, s].astype(F32)
+            zs[n, g, :, i] = total.astype(BF).reshape(nz, shard, BLOCK)
+        all_along(z_copy, n, g)
+        zr[n, g, z] = zs[n, g, z]
+
+    def z_total(n, g):
+        wait_along(z_arr, n, g)
+        return jnp.sum(zr[n, g].astype(F32), axis=0)
+
+    def c_pass(n, g):
+        wait_along(c_arr, n, g)
+        cx_copy(n, g, x_lo).start()
+
+    def blocks(n, g, i):
+        return [cz[n, g, b, :, i].reshape(SLOTS, BLOCK) for b in range(2)]
+
+    def unpack(two, dst, s):
+        zero = jnp.zeros((SLOTS, BLOCK), BF)
+        wide = jnp.concatenate(
+            [jnp.concatenate([two[0], zero], axis=1), jnp.concatenate([zero, two[1]], axis=1)], axis=0
+        )
+        dst[:, s * lats : (s + 1) * lats] = dot(selt[s], wide).astype(BF)
+
+    up = [(0, 1), (2, 3)]
+    down = [(3, 2), (1, 0)]
 
     for s in range(layers):
         dense = dot(xg[:, first(s) : first(s) + span], encp[s]).astype(BF)
-        pack(dense, pk, s)
-        scatter(pk, rx, s, 0)
-
-    for n in range(width // LANE):
-        xt[n * LANE : (n + 1) * LANE, :] = xg[:, n * LANE : (n + 1) * LANE].T
-
-    b_of = q * shard // SLOTS
-    for s in range(layers):
-        lat_wait(lat_r, s, 0)
-        total = jnp.sum(rx[s].astype(F32), axis=0)
-        bias = jnp.where(b_of == 0, bias_in[s : s + 1, 0:BLOCK], bias_in[s : s + 1, BLOCK : 2 * BLOCK])
-        pre = total + bias
-        small = jnp.exp(-jnp.abs(pre))
-        ck[s, lat_rows(q), :] = (jnp.maximum(pre, 0.0) + jnp.log1p(small)).astype(BF)
-        slope[s] = jnp.where(pre >= 0, 1.0, small) / (1.0 + small)
-        spread(ck, s, 1)
-
-    def unpack(src, dst, s):
-        zero = jnp.zeros((SLOTS, BLOCK), BF)
-        wide = jnp.concatenate(
-            [
-                jnp.concatenate([src[s, 0:SLOTS, :], zero], axis=1),
-                jnp.concatenate([zero, src[s, SLOTS : 2 * SLOTS, :]], axis=1),
-            ],
-            axis=0,
-        )
-        dst[:, s * lats : (s + 1) * lats] = dot(selt[s], wide).astype(BF)
-
-    for s in range(layers):
-        lat_wait(lat_r, s, 1)
-        unpack(ck, cd, s)
-
+        pack(dense, 0, s)
+    for g, members in enumerate(up):
+        z_send(0, g, members)
+    for g, members in enumerate(up):
+        total = z_total(0, g)
+        for i, s in enumerate(members):
+            bias = jnp.where(x_lo == 0, bias_in[s : s + 1, 0:BLOCK], bias_in[s : s + 1, BLOCK : 2 * BLOCK])
+            pre = total[i] + bias
+            small = jnp.exp(-jnp.abs(pre))
+            cz[0, g, x_lo, z, i] = (jnp.maximum(pre, 0.0) + jnp.log1p(small)).astype(BF)
+            slope[s] = jnp.where(pre >= 0, 1.0, small) / (1.0 + small)
+        all_along(c_copy, 0, g)
+    for g in range(2):
+        c_pass(0, g)
     for copy in dec_loads:
         copy.wait()
+
+    def codes(g):
+        cx_copy(0, g, 1 - x_lo).wait_recv()
+        for i, s in enumerate(up[g]):
+            unpack(blocks(0, g, i), cd, s)
 
     tiles = [min(layers, ((n + 1) * LANE - 1) // dl + 1) for n in range(width // LANE)]
     groups = []
@@ -362,15 +386,12 @@
     def lanes_of(c):
         return pl.ds(cuts[c][0], cuts[c][1] - cuts[c][0])
 
-    hm_copies = []
-    for c in range(nc):
-        decode(1 - core, hm_s, c)
-        hm_copies.append(
-            pltpu.make_async_remote_copy(
-                hm_s.at[:, lanes_of(c)], hm_r.at[:, lanes_of(c)], hm_sem.at[0, c], hm_sem.at[1, c], device_id=mate
-            )
+    hm_copies = [
+        pltpu.make_async_remote_copy(
+            hm_s.at[:, lanes_of(c)], hm_r.at[:, lanes_of(c)], hm_sem.at[0, c], hm_sem.at[1, c], device_id=mate
         )
-        hm_copies[c].start()
+        for c in range(nc)
+    ]
 
     def mine(offset, c):
         return ho[local(offset), lanes_of(c)] + hm_r[local(offset), lanes_of(c)].astype(F32)
@@ -397,10 +418,23 @@
         buf_s[i, :, lanes_of(c)] = part.astype(BF)
         copies[i][c].start()
 
+    early = [c for c in range(nc) if max(n for lo, _, n in groups if lo * LANE < cuts[c][1]) <= len(up[0])]
+    codes(0)
+    for c in early:
+        decode(1 - core, hm_s, c)
+        hm_copies[c].start()
+        decode(core, ho, c)
+    codes(1)
     for i in range(na):
+        if i == 0:
+            for c in range(nc):
+                if c not in early:
+                    decode(1 - core, hm_s, c)
+                    hm_copies[c].start()
         for c in range(nc):
             if i == 0:
-                decode(core, ho, c)
+                if c not in early:
+                    decode(core, ho, c)
                 hm_copies[c].wait_recv()
             forward(a_copies, ra_s, ra_r, i, na - i, c)
             if i < nb:
@@ -439,42 +473,51 @@
     def _():
         rec_copy.start()
 
-    gather_run(e_copies, [])
-
-    for s in range(layers - 1, -1, -1):
-        low = dl * s // LANE * LANE
-        dense = dot(eg[:, low:width], dcat[low:width, s * lats : (s + 1) * lats]).astype(BF)
-        pack(dense, pc, s)
-        scatter(pc, rc, s, 2)
-
-    for n in range(width // LANE):
-        et[n * LANE : (n + 1) * LANE, :] = eg[:, n * LANE : (n + 1) * LANE].T
+    def turn(buf, out, n):
+        out[n * LANE : (n + 1) * LANE, :] = buf[:, n * LANE : (n + 1) * LANE].T
+
+    def turn_inputs(i):
+        for n in range(width // LANE):
+            if n % na == i:
+                turn(xg, xt, n)
+
+    gather_run(e_copies, [functools.partial(turn_inputs, i) for i in range(na)])
+
+    for group in down:
+        for s in group:
+            low = dl * s // LANE * LANE
+            dense = dot(eg[:, low:width], dcat[low:width, s * lats : (s + 1) * lats]).astype(BF)
+            pack(dense, 1, s)
 
     def decoder_grad(t):
         out = dot(et[t * dl : (t + 1) * dl, :], cd[:, 0 : (t + 1) * lats])
         for s in range(t + 1):
             dg_ref[t * (t + 1) // 2 + s] = out[:, s * lats : (s + 1) * lats].astype(BF)
 
+    for g, members in enumerate(down):
+        z_send(1, g, members)
+    for n in range(width // LANE):
+        turn(eg, et, n)
     decoder_grad(0)
+    for g, members in enumerate(down):
+        total = z_total(1, g)
+        for i, s in enumerate(members):
+            cz[1, g, x_lo, z, i] = (total[i] * slope[s]).astype(BF)
+        all_along(c_copy, 1, g)
     decoder_grad(1)
-
-    for s in range(layers - 1, -1, -1):
-        lat_wait(lat_r, s, 2)
-        total = jnp.sum(rc[s].astype(F32), axis=0)
-        pg[s, lat_rows(q), :] = (total * slope[s]).astype(BF)
-        spread(pg, s, 3)
-
     decoder_grad(2)
+    for g in range(2):
+        c_pass(1, g)
     decoder_grad(3)
 
-    for s in range(layers - 1, -1, -1):
-        lat_wait(lat_r, s, 3)
-        unpack(pg, pgd, s)
-        for b in range(2):
-            bg_ref[s : s + 1, b * BLOCK : (b + 1) * BLOCK] = jnp.sum(
-                pg[s, b * SLOTS : (b + 1) * SLOTS, :].astype(F32), axis=0, keepdims=True
-            )
-        eg_ref[s] = dot(xt[s * dl : (s + 1) * dl, :], pgd[:, s * lats : (s + 1) * lats]).astype(BF)
+    for g, members in enumerate(down):
+        cx_copy(1, g, 1 - x_lo).wait_recv()
+        for i, s in enumerate(members):
+            two = blocks(1, g, i)
+            unpack(two, pgd, s)
+            for b in range(2):
+                bg_ref[s : s + 1, b * BLOCK : (b + 1) * BLOCK] = jnp.sum(two[b].astype(F32), axis=0, keepdims=True)
+            eg_ref[s] = dot(xt[s * dl : (s + 1) * dl, :], pgd[:, s * lats : (s + 1) * lats]).astype(BF)
 
     @pl.when(owner)
     def _():
@@ -501,9 +544,13 @@
             copy.wait_send()
     gather_end(x_copies)
     gather_end(e_copies)
-    for n in range(4):
+    for n in range(2):
         for s in range(layers):
-            lat_wait(lat_s, s, n)
+            x_copy(n, s).wait_send()
+        for g in range(2):
+            wait_along(z_out, n, g)
+            wait_along(c_out, n, g)
+            cx_copy(n, g, x_lo).wait_send()
 
 
 def step(sizes, layer_inputs, layer_outputs, encoder, encoder_bias, decoder, active_blocks):
@@ -511,7 +558,8 @@
     width = layers * dl
     places = 2 * ny * chunk
     na, nb = ny // 2, max(1, ny // 2 - 1)
-    shard = 2 * SLOTS // nl
+    nz = nl // 2
+    shard = SLOTS // nz
     pairs = decoder.shape[0]
     vmem, dma = pltpu.VMEM, pltpu.SemaphoreType.DMA
     ring = (chunk, width)
@@ -528,12 +576,12 @@
         vmem((layers, places, 2 * SLOTS), BF),
         vmem((2, 32, width), BF),
         vmem((2, 2, 32, width), BF),
-        vmem((layers, 2 * SLOTS, BLOCK), BF),
-        vmem((layers, nl, shard, BLOCK), BF),
-        vmem((layers, 2 * SLOTS, BLOCK), BF),
-        vmem((layers, 2 * SLOTS, BLOCK), BF),
-        vmem((layers, nl, shard, BLOCK), BF),
-        vmem((layers, 2 * SLOTS, BLOCK), BF),
+        vmem((2, layers, SLOTS, BLOCK), BF),
+        vmem((2, layers, SLOTS, BLOCK), BF),
+        vmem((2, layers, SLOTS, BLOCK), F32),
+        vmem((2, 2, nz, layers // 2, shard, BLOCK), BF),
+        vmem((2, 2, nz, layers // 2, shard, BLOCK), BF),
+        vmem((2, 2, 2, nz, layers // 2, shard, BLOCK), BF),
         vmem((layers, shard, BLOCK), F32),
         vmem((places // 2, width), BF),
         vmem((places // 2, width), BF),
@@ -559,8 +607,14 @@
         dma((2, nb, 3)),
         dma((2, ny)),
         dma((2, ny)),
-        dma((4, layers)),
-        dma((4, layers)),
+        dma((2, layers)),
+        dma((2, layers)),
+        dma((2, 2)),
+        dma((2, 2)),
+        dma((2, 2)),
+        dma((2, 2)),
+        dma((2, 2)),
+        dma((2, 2)),
         dma((2, 3)),
         dma((na, 3)),
         dma((na, 3)),
@@ -570,7 +624,6 @@
         dma((2,)),
     ]
     in_vmem = pl.BlockSpec(memory_space=pltpu.VMEM)
-    anywhere = pl.BlockSpec(memory_space=pl.ANY)
     rec, eg, bg, dg = pl.pallas_call(
         functools.partial(kernel, sizes),
         out_shape=(
@@ -579,11 +632,11 @@
             jax.ShapeDtypeStruct((layers, lats), F32),
             jax.ShapeDtypeStruct((pairs, dl, lats), BF),
         ),
-        in_specs=[anywhere] * 6,
+        in_specs=[pl.BlockSpec(memory_space=pltpu.HBM)] * 6,
         out_specs=(in_vmem,) * 4,
         scratch_shapes=scratch,
         compiler_params=pltpu.CompilerParams(
-            collective_id=0, has_side_effects=True, vmem_limit_bytes=60 * 1024 * 1024
+            collective_id=0, has_side_effects=True, vmem_limit_bytes=56 * 1024 * 1024
         ),
     )(
         layer_inputs.transpose(2, 0, 1),

time: 112 us -> 116 us (1.036)
  Pallas kernels: 104 us -> 108 us
    pallas_call x1, Pallas kernels: 104 us -> 108 us  [step(): pl.pallas_call(functools.partial(kernel, sizes), out_shape=(jax.ShapeDtyp...]
where the time goes in v3:
time: 116 us
  Pallas kernels  108 us (93%)
  local copies, waits for them, and re-layouts  6.93 us (6%)
    pallas_call x1, Pallas kernels, step(): pl.pallas_call(functools.partial(kernel, sizes), out_shape=(jax.ShapeDtyp...  108 us
    unnamed x3, local copies, waits for them, and re-layouts  5.42 us

profile of v3, /device:TPU:1, one launch (start us, length us, event | category | flops | bytes accessed | tf_op | source)
XLA Modules:
  0.0 115.9 jit_solution(17398894389489793126)
XLA Ops:
  0.6 108.4 %shard_map.93 = (bf16[22,896]{1,0:T(8,128)(2,1)}, bf16[4,224,256]{2,1,0:T(8,128)(2,1)}, f32[4,256]{1,0:T(4,128)}, bf16[10,224,256]{2,1,0:T(8,128)(2,1)}) custom-call(bf16[22,4,224]{2,1,0:T(4,128)(2,1)} %bitcast.2, bf16[22,4,224]{2,1,0:T(4,128)(2,1)} %y_ref.1, bf16[4,224,256]{2,1,0:T(8,128)(2,1)} %enc_ref.1, f32[4,256]{1,0:T(4,128)} %bias_ref.1, ...), custom_call_target="tpu_custom_call" | custom-call | tf_op jit(solution)/shard_map/pallas_call | solution.py:627
  109.0 1.5 %reshape.11 = bf16[22,4,224]{2,1,0:T(4,128)(2,1)} reshape(bf16[22,896]{1,0:T(8,128)(2,1)} %get-tuple-element.8) | data formatting | bytes 78848 | tf_op jit(solution)/shard_map/reshape | solution.py:649
  110.5 1.8 %copy.13 = bf16[4,224,256]{2,1,0:T(8,128)(2,1)} copy(bf16[4,224,256]{2,1,0:T(8,128)(2,1)} %get-tuple-element.17) | data formatting | bytes 917504
  112.3 1.3 %copy.14 = f32[4,256]{1,0:T(4,128)} copy(f32[4,256]{1,0:T(4,128)} %get-tuple-element.18) | data formatting | bytes 8192
  113.6 2.3 %copy.15 = bf16[10,224,256]{2,1,0:T(8,128)(2,1)} copy(bf16[10,224,256]{2,1,0:T(8,128)(2,1)} %get-tuple-element.19) | data formatting | bytes 2293760

commit v4 on v2

--- a/solution.py
+++ b/solution.py
@@ -11,6 +11,7 @@
 ROWBLOCK = 32
 MOST = 4
 SLOTS = MOST * ROWBLOCK
+TILE = 16
 LANE = 128
 BF, F32 = jnp.bfloat16, jnp.float32
 
@@ -29,9 +30,9 @@
     rec_ref, eg_ref, bg_ref, dg_ref,
     xg, eg, xt, et, cd, pgd, encp, dcat, sel, selt,
     xy_s, xy_r, pk, rx, ck, pc, rc, pg, slope,
-    hm_s, hm_r, ho, ra_s, ra_r, rb_s, rb_r, fx_s, fx_r, recb, yc, x_in, y_in, act_in, bias_in,
-    load_sem, xy_out, xy_sem, ag_as, ag_ar, ag_bs, ag_br, ag_ms, ag_mr,
-    lat_s, lat_r, hm_sem, rs_as, rs_ar, rs_bs, rs_br, fx_sem, rec_sem,
+    hm_s, hm_r, ho, ra_s, ra_r, rb_s, rb_r, fx_s, fx_r, recb, yc, x_in, y_in, act_in, bias_in, bsum, egb, dgb,
+    load_sem, xy_out, xy_sem, ag_out, ag_ar, ag_br, ag_mr,
+    lat_s, lat_r, hm_sem, rs_out, rs_ar, rs_br, fx_out, fx_sem, rec_sem, out_sem,
 ):
     layers, dl, lats, rows, ny, nl, chunk = sizes
     width = layers * dl
@@ -60,8 +61,18 @@
         slot = lax.rem(y + step * offset + 2 * ny, ny)
         return pl.ds(pl.multiple_of((hh * ny + slot) * chunk, 16), chunk)
 
-    def local(offset):
-        return place(0, offset)
+    tiles = chunk // TILE
+
+    def tile_of(hh, offset, c):
+        slot = lax.rem(y + step * offset + 2 * ny, ny)
+        return pl.ds(pl.multiple_of((hh * ny + slot) * chunk + c * TILE, TILE), TILE)
+
+    def loop(count, body):
+        def one(i, carry):
+            body(i)
+            return carry
+
+        lax.fori_loop(0, count, one, 0)
 
     diagonal = at(1 - h, y, 1 - core)
 
@@ -151,80 +162,71 @@
 
         return merged(n)
 
-    cuts = [(0, 3 * LANE), (3 * LANE, 5 * LANE), (5 * LANE, width)]
-    nc = len(cuts)
-
     def gather_copies(buf, n):
-        def ring(to, offset, send, recv, lanes):
-            where = buf.at[place(core, offset), pl.ds(lanes[0], lanes[1] - lanes[0])]
+        def piece(to, offset, send, recv, c):
+            where = buf.at[tile_of(core, offset, c)]
             return pltpu.make_async_remote_copy(where, where, send, recv, device_id=to)
 
-        def rings(to, sign, shift, count, send, recv):
-            return [
-                [ring(to, sign * (i + shift), send.at[n, i, c], recv.at[n, i, c], cuts[c]) for c in range(nc)]
-                for i in range(count)
-            ]
-
-        a_out, a_in = rings(to_a, -1, 0, na, ag_as, ag_ar), rings(to_a, -1, 1, na, ag_as, ag_ar)
-        b_out, b_in = rings(to_b, 1, 0, nb, ag_bs, ag_br), rings(to_b, 1, 1, nb, ag_bs, ag_br)
+        def a_out(i, c):
+            return piece(to_a, -i, ag_out.at[n], ag_ar.at[n, i, c], c)
+
+        def b_out(i, c):
+            return piece(to_b, i, ag_out.at[n], ag_br.at[n, i, c], c)
+
+        def a_in(i, c):
+            return piece(to_a, -i - 1, ag_out.at[n], ag_ar.at[n, i, c], c)
+
+        def b_in(i, c):
+            return piece(to_b, i + 1, ag_out.at[n], ag_br.at[n, i, c], c)
+
         order = [0]
         for i in range(na):
             order.append(-i - 1)
             if i < nb:
                 order.append(i + 1)
-        pass_on, from_mate = [], []
-        for j, o in enumerate(order):
-            where = buf.at[place(core, o)]
-            pass_on.append(
-                pltpu.make_async_remote_copy(where, where, ag_ms.at[n, j], ag_mr.at[n, j], device_id=mate)
-            )
-            where = buf.at[place(1 - core, -o)]
-            from_mate.append(
-                pltpu.make_async_remote_copy(where, where, ag_ms.at[n, j], ag_mr.at[n, j], device_id=mate)
-            )
+
+        def pass_on(j):
+            where = buf.at[place(core, order[j])]
+            return pltpu.make_async_remote_copy(where, where, ag_out.at[n], ag_mr.at[n, j], device_id=mate)
+
+        def from_mate(j):
+            where = buf.at[place(1 - core, -order[j])]
+            return pltpu.make_async_remote_copy(where, where, ag_out.at[n], ag_mr.at[n, j], device_id=mate)
+
         return a_out, b_out, a_in, b_in, pass_on, from_mate
 
     def gather_start(copies, c):
-        copies[0][0][c].start()
+        copies[0](0, c).start()
         if nb:
-            copies[1][0][c].start()
+            copies[1](0, c).start()
 
     def gather_run(copies, extra):
         a_out, b_out, a_in, b_in, pass_on, from_mate = copies
-        pass_on[0].start()
+        pass_on(0).start()
         j = 1
         for i in range(na):
-            for c in range(nc):
-                a_in[i][c].wait_recv()
+
+            def advance(c):
+                a_in(i, c).wait_recv()
                 if i + 1 < na:
-                    a_out[i + 1][c].start()
+                    a_out(i + 1, c).start()
                 if i < nb:
-                    b_in[i][c].wait_recv()
+                    b_in(i, c).wait_recv()
                     if i + 1 < nb:
-                        b_out[i + 1][c].start()
+                        b_out(i + 1, c).start()
+
+            loop(tiles, advance)
             for _ in range(2 if i < nb else 1):
-                pass_on[j].start()
+                pass_on(j).start()
                 j += 1
             if i < len(extra):
                 extra[i]()
-        for more in extra[na:]:
-            more()
-        for copy in from_mate:
-            copy.wait_recv()
-
-    def gather_end(copies):
-        a_out, b_out, a_in, b_in, pass_on, from_mate = copies
-        for group in a_out + b_out:
-            for copy in group:
-                copy.wait_send()
-        for copy in pass_on:
-            copy.wait_send()
-
-    own = place(core, 0)
-    x_copies = gather_copies(xg, 0)
-    xg[own, :] = xy_arrive(0)
-    for c in range(nc):
-        gather_start(x_copies, c)
+        for j in range(ny):
+            from_mate(j).wait_recv()
+
+    def sent(buf, rows_sent, sem):
+        where = buf.at[pl.ds(0, rows_sent)]
+        pltpu.make_async_copy(where, where, sem).wait()
 
     nr = act_in.shape[2]
     ii, jj = iota((nr, nr), 0), iota((nr, nr), 1)
@@ -258,16 +260,26 @@
             want = jnp.sum(jnp.where(rank_row == col_rank, col_value, 0.0), axis=1, keepdims=True) - 1.0
             want_row = jnp.sum(jnp.where(rank == row_rank, row_value, 0.0), axis=0, keepdims=True) - 1.0
             sel[s, b * SLOTS : (b + 1) * SLOTS, :] = jnp.where(want == lane_row, 1.0, 0.0).astype(BF)
-            for c in range(2 * ny):
-                selt[s, c * chunk : (c + 1) * chunk, b * SLOTS : (b + 1) * SLOTS] = jnp.where(
-                    chip_row == want_row - float(c * real), 1.0, 0.0
+
+            def chip(c):
+                here = pl.ds(pl.multiple_of(c * chunk, TILE), chunk)
+                selt[s, here, b * SLOTS : (b + 1) * SLOTS] = jnp.where(
+                    chip_row == want_row - (c * real).astype(F32), 1.0, 0.0
                 ).astype(BF)
+
+            loop(2 * ny, chip)
 
     def outputs():
         yc[...] = xy_arrive(1)
 
-    choose(0)
-    gather_run(x_copies, [functools.partial(choose, s) for s in range(1, layers)] + [outputs])
+    loop(layers, choose)
+
+    own = place(core, 0)
+    x_copies = gather_copies(xg, 0)
+    xg[own, :] = xy_arrive(0)
+    loop(tiles, functools.partial(gather_start, x_copies))
+
+    gather_run(x_copies, [outputs])
     for copy in enc_loads:
         copy.wait()
 
@@ -306,24 +318,38 @@
             part = slice(b * SLOTS, (b + 1) * SLOTS)
             dst[s, part, :] = both[part, b * BLOCK : (b + 1) * BLOCK].astype(BF)
 
-    for s in range(layers):
-        dense = dot(xg[:, first(s) : first(s) + span], encp[s]).astype(BF)
+    def lane_block(s):
+        return pl.ds(pl.multiple_of(s * lats, LANE), lats)
+
+    def encode(s):
+        start = jnp.minimum(dl * s // LANE * LANE, width - span)
+        dense = dot(xg[:, pl.ds(pl.multiple_of(start, LANE), span)], encp[s]).astype(BF)
         pack(dense, pk, s)
         scatter(pk, rx, s, 0)
 
-    for n in range(width // LANE):
-        xt[n * LANE : (n + 1) * LANE, :] = xg[:, n * LANE : (n + 1) * LANE].T
+    loop(layers, encode)
+
+    def turn(src, out):
+        def one(n):
+            here = pl.ds(pl.multiple_of(n * LANE, LANE), LANE)
+            out[here, :] = src[:, here].T
+
+        loop(width // LANE, one)
+
+    turn(xg, xt)
 
     b_of = q * shard // SLOTS
-    for s in range(layers):
+    def activate(s):
         lat_wait(lat_r, s, 0)
         total = jnp.sum(rx[s].astype(F32), axis=0)
-        bias = jnp.where(b_of == 0, bias_in[s : s + 1, 0:BLOCK], bias_in[s : s + 1, BLOCK : 2 * BLOCK])
-        pre = total + bias
+        bias = bias_in[pl.ds(s, 1), :]
+        pre = total + jnp.where(b_of == 0, bias[:, 0:BLOCK], bias[:, BLOCK : 2 * BLOCK])
         small = jnp.exp(-jnp.abs(pre))
         ck[s, lat_rows(q), :] = (jnp.maximum(pre, 0.0) + jnp.log1p(small)).astype(BF)
         slope[s] = jnp.where(pre >= 0, 1.0, small) / (1.0 + small)
         spread(ck, s, 1)
+
+    loop(layers, activate)
 
     def unpack(src, dst, s):
         zero = jnp.zeros((SLOTS, BLOCK), BF)
@@ -334,104 +360,110 @@
             ],
             axis=0,
         )
-        dst[:, s * lats : (s + 1) * lats] = dot(selt[s], wide).astype(BF)
-
-    for s in range(layers):
+        dst[:, lane_block(s)] = dot(selt[s], wide).astype(BF)
+
+    def codes(s):
         lat_wait(lat_r, s, 1)
         unpack(ck, cd, s)
 
+    loop(layers, codes)
+
     for copy in dec_loads:
         copy.wait()
 
-    tiles = [min(layers, ((n + 1) * LANE - 1) // dl + 1) for n in range(width // LANE)]
     groups = []
-    for n, count in enumerate(tiles):
+    for n in range(width // LANE):
+        count = min(layers, ((n + 1) * LANE - 1) // dl + 1)
         if groups and groups[-1][2] == count:
             groups[-1][1] = n + 1
         else:
             groups.append([n, n + 1, count])
 
-    def decode(hh, out, c):
-        base = pl.ds(pl.multiple_of(hh * half, 16), half)
+    hm_copy = pltpu.make_async_remote_copy(hm_s, hm_r, hm_sem.at[0], hm_sem.at[1], device_id=mate)
+
+    def decode(j):
+        hh = jnp.where(j == 0, 1 - core, core)
+        base = pl.ds(pl.multiple_of(hh * half, TILE), half)
         for lo, hi, count in groups:
-            if cuts[c][0] <= lo * LANE < cuts[c][1]:
-                lanes = slice(lo * LANE, hi * LANE)
-                part = dot(cd[base, 0 : count * lats], dcat[lanes, 0 : count * lats], ((1,), (1,)))
-                out[:, lanes] = part.astype(out.dtype)
-
-    def lanes_of(c):
-        return pl.ds(cuts[c][0], cuts[c][1] - cuts[c][0])
-
-    hm_copies = []
-    for c in range(nc):
-        decode(1 - core, hm_s, c)
-        hm_copies.append(
-            pltpu.make_async_remote_copy(
-                hm_s.at[:, lanes_of(c)], hm_r.at[:, lanes_of(c)], hm_sem.at[0, c], hm_sem.at[1, c], device_id=mate
-            )
+            lanes = slice(lo * LANE, hi * LANE)
+            ho[:, lanes] = dot(cd[base, 0 : count * lats], dcat[lanes, 0 : count * lats], ((1,), (1,)))
+
+        @pl.when(j == 0)
+        def _():
+            hm_s[...] = ho[...].astype(BF)
+            hm_copy.start()
+
+    loop(2, decode)
+    hm_copy.wait_recv()
+
+    def mine(offset, c):
+        where = tile_of(0, offset, c)
+        return ho[where, :] + hm_r[where, :].astype(F32)
+
+    def small_tile(c):
+        return pl.ds(pl.multiple_of(c * TILE, TILE), TILE)
+
+    def a_copy(i, c):
+        return pltpu.make_async_remote_copy(
+            ra_s.at[i, small_tile(c)], ra_r.at[i, small_tile(c)], rs_out.at[0], rs_ar.at[i, c], device_id=to_a
         )
-        hm_copies[c].start()
-
-    def mine(offset, c):
-        return ho[local(offset), lanes_of(c)] + hm_r[local(offset), lanes_of(c)].astype(F32)
-
-    def sums(to, count, buf_s, buf_r, send, recv):
-        return [
-            [
-                pltpu.make_async_remote_copy(
-                    buf_s.at[i, :, lanes_of(c)], buf_r.at[i, :, lanes_of(c)], send.at[i, c], recv.at[i, c], device_id=to
-                )
-                for c in range(nc)
-            ]
-            for i in range(count)
-        ]
-
-    a_copies = sums(to_a, na, ra_s, ra_r, rs_as, rs_ar)
-    b_copies = sums(to_b, nb, rb_s, rb_r, rs_bs, rs_br)
-
-    def forward(copies, buf_s, buf_r, i, offset, c):
+
+    def b_copy(i, c):
+        return pltpu.make_async_remote_copy(
+            rb_s.at[i, small_tile(c)], rb_r.at[i, small_tile(c)], rs_out.at[0], rs_br.at[i, c], device_id=to_b
+        )
+
+    def forward(copy, buf_s, buf_r, i, offset, c):
         part = mine(offset, c)
         if i:
-            copies[i - 1][c].wait_recv()
-            part = part + buf_r[i - 1, :, lanes_of(c)].astype(F32)
-        buf_s[i, :, lanes_of(c)] = part.astype(BF)
-        copies[i][c].start()
+            copy(i - 1, c).wait_recv()
+            part = part + buf_r[i - 1, small_tile(c), :].astype(F32)
+        buf_s[i, small_tile(c), :] = part.astype(BF)
+        copy(i, c).start()
 
     for i in range(na):
-        for c in range(nc):
-            if i == 0:
-                decode(core, ho, c)
-                hm_copies[c].wait_recv()
-            forward(a_copies, ra_s, ra_r, i, na - i, c)
+
+        def both(c):
+            forward(a_copy, ra_s, ra_r, i, na - i, c)
             if i < nb:
-                forward(b_copies, rb_s, rb_r, i, i - nb, c)
-    fx_copies = []
-    for c in range(nc):
+                forward(b_copy, rb_s, rb_r, i, i - nb, c)
+
+        loop(tiles, both)
+
+    def fx_copy(c):
+        here = small_tile(c)
+        return pltpu.make_async_remote_copy(
+            fx_s.at[here], fx_r.at[here], fx_out.at[0], fx_sem.at[c], device_id=partner
+        )
+
+    def finish(c):
+        here = small_tile(c)
         total = mine(0, c)
-        a_copies[na - 1][c].wait_recv()
-        total = total + ra_r[na - 1, :, lanes_of(c)].astype(F32)
+        a_copy(na - 1, c).wait_recv()
+        total = total + ra_r[na - 1, here, :].astype(F32)
         if nb:
-            b_copies[nb - 1][c].wait_recv()
-            total = total + rb_r[nb - 1, :, lanes_of(c)].astype(F32)
-        fx_s[:, lanes_of(c)] = total.astype(BF)
-        fx_copies.append(
-            pltpu.make_async_remote_copy(
-                fx_s.at[:, lanes_of(c)], fx_r.at[:, lanes_of(c)], fx_sem.at[0, c], fx_sem.at[1, c], device_id=partner
-            )
-        )
-        fx_copies[c].start()
+            b_copy(nb - 1, c).wait_recv()
+            total = total + rb_r[nb - 1, here, :].astype(F32)
+        fx_s[here, :] = total.astype(BF)
+        fx_copy(c).start()
+
+    loop(tiles, finish)
 
     e_copies = gather_copies(eg, 1)
-    for c in range(nc):
-        fx_copies[c].wait_recv()
-        lanes = lanes_of(c)
-        whole = fx_s[:, lanes].astype(F32) + fx_r[:, lanes].astype(F32)
-        eg[own, lanes] = (whole - yc[:, lanes].astype(F32)).astype(BF)
+
+    def differ(c):
+        here = small_tile(c)
+        fx_copy(c).wait_recv()
+        whole = fx_s[here, :].astype(F32) + fx_r[here, :].astype(F32)
+        eg[tile_of(core, 0, c), :] = (whole - yc[here, :].astype(F32)).astype(BF)
         gather_start(e_copies, c)
-
-        @pl.when(owner)
-        def _():
-            recb[:, lanes] = whole.astype(BF)
+        ho[here, :] = whole
+
+    loop(tiles, differ)
+
+    @pl.when(owner)
+    def _():
+        recb[...] = ho[0:chunk, :].astype(BF)
 
     rec_copy = pltpu.make_async_remote_copy(recb, recb, rec_sem.at[0], rec_sem.at[1], device_id=mate)
 
@@ -441,40 +473,51 @@
 
     gather_run(e_copies, [])
 
-    for s in range(layers - 1, -1, -1):
-        low = dl * s // LANE * LANE
-        dense = dot(eg[:, low:width], dcat[low:width, s * lats : (s + 1) * lats]).astype(BF)
+    def out_copy(buf, ref, n, sem):
+        return pltpu.make_async_copy(buf.at[n], ref.at[n], out_sem.at[sem])
+
+    def back(s):
+        dense = dot(eg[...], dcat[:, lane_block(s)]).astype(BF)
         pack(dense, pc, s)
         scatter(pc, rc, s, 2)
 
-    for n in range(width // LANE):
-        et[n * LANE : (n + 1) * LANE, :] = eg[:, n * LANE : (n + 1) * LANE].T
-
-    def decoder_grad(t):
-        out = dot(et[t * dl : (t + 1) * dl, :], cd[:, 0 : (t + 1) * lats])
-        for s in range(t + 1):
-            dg_ref[t * (t + 1) // 2 + s] = out[:, s * lats : (s + 1) * lats].astype(BF)
-
-    decoder_grad(0)
-    decoder_grad(1)
-
-    for s in range(layers - 1, -1, -1):
+    loop(layers, back)
+    turn(eg, et)
+
+    def decoder_grad(pair):
+        t = jnp.int32(0)
+        for n in range(1, layers):
+            t = t + jnp.where(pair >= n * (n + 1) // 2, 1, 0)
+        s = pair - t * (t + 1) // 2
+        out = dot(et[pl.ds(pl.multiple_of(t * dl, TILE), dl), :], cd[:, lane_block(s)])
+        dgb[pair] = out.astype(BF)
+        out_copy(dgb, dg_ref, pair, layers + pair).start()
+
+    pairs = dg_ref.shape[0]
+    loop(pairs // 3, decoder_grad)
+
+    def settle(s):
         lat_wait(lat_r, s, 2)
         total = jnp.sum(rc[s].astype(F32), axis=0)
         pg[s, lat_rows(q), :] = (total * slope[s]).astype(BF)
         spread(pg, s, 3)
 
-    decoder_grad(2)
-    decoder_grad(3)
-
-    for s in range(layers - 1, -1, -1):
+    loop(layers, settle)
+    loop(pairs - pairs // 3, lambda n: decoder_grad(n + pairs // 3))
+
+    def encoder_grad(s):
         lat_wait(lat_r, s, 3)
         unpack(pg, pgd, s)
         for b in range(2):
-            bg_ref[s : s + 1, b * BLOCK : (b + 1) * BLOCK] = jnp.sum(
+            bsum[s, :, b * BLOCK : (b + 1) * BLOCK] = jnp.sum(
                 pg[s, b * SLOTS : (b + 1) * SLOTS, :].astype(F32), axis=0, keepdims=True
             )
-        eg_ref[s] = dot(xt[s * dl : (s + 1) * dl, :], pgd[:, s * lats : (s + 1) * lats]).astype(BF)
+        egb[s] = dot(xt[pl.ds(pl.multiple_of(s * dl, TILE), dl), :], pgd[:, lane_block(s)]).astype(BF)
+        out_copy(egb, eg_ref, s, s).start()
+
+    loop(layers, encoder_grad)
+    for s in range(layers):
+        bg_ref[s : s + 1, :] = bsum[s]
 
     @pl.when(owner)
     def _():
@@ -485,7 +528,9 @@
         rec_copy.wait_recv()
 
     take = jnp.where(iota((rows, chunk), 1) == iota((rows, chunk), 0) + rows * core, 1.0, 0.0).astype(BF)
-    rec_ref[...] = dot(take, recb[...]).astype(BF)
+    out = dot(take, recb[...]).astype(BF)
+    for t in range(layers):
+        rec_ref[:, t, :] = out[:, t * dl : (t + 1) * dl]
 
     for n in range(2):
         xy_copy(n, mate, core).wait_send()
@@ -494,16 +539,32 @@
         def _():
             xy_copy(n, mate, 1 - core).wait_send()
 
-    for copy in hm_copies + fx_copies:
-        copy.wait_send()
-    for group in a_copies + b_copies:
-        for copy in group:
-            copy.wait_send()
-    gather_end(x_copies)
-    gather_end(e_copies)
+    loop(layers, lambda s: out_copy(egb, eg_ref, s, s).wait())
+    loop(pairs, lambda n: out_copy(dgb, dg_ref, n, layers + n).wait())
+    hm_copy.wait_send()
+    sent(xg, chunk, fx_out.at[0])
+    sent(xg, (na + nb) * chunk, rs_out.at[0])
+    for n in range(2):
+        sent(xg, (na + nb + ny) * chunk, ag_out.at[n])
     for n in range(4):
         for s in range(layers):
             lat_wait(lat_s, s, n)
+
+
+def hand_over(*refs):
+    count = (len(refs) - 1) // 2
+    sem = refs[-1]
+    copies = []
+    for n in range(count):
+        src, dst = refs[n], refs[count + n]
+        parts = src.shape[0] if n in (1, 3) else 1
+        for p in range(parts):
+            pair = (src.at[p], dst.at[p]) if parts > 1 else (src, dst)
+            copies.append(pltpu.make_async_copy(*pair, sem.at[len(copies)]))
+    for copy in copies:
+        copy.start()
+    for copy in copies:
+        copy.wait()
 
 
 def step(sizes, layer_inputs, layer_outputs, encoder, encoder_bias, decoder, active_blocks):
@@ -514,7 +575,7 @@
     shard = 2 * SLOTS // nl
     pairs = decoder.shape[0]
     vmem, dma = pltpu.VMEM, pltpu.SemaphoreType.DMA
-    ring = (chunk, width)
+    ring, tiles = (chunk, width), chunk // TILE
     scratch = [
         vmem((places, width), BF),
         vmem((places, width), BF),
@@ -550,40 +611,42 @@
         vmem((rows, layers, dl), BF),
         vmem((layers, active_blocks.shape[2], active_blocks.shape[1]), jnp.int32),
         vmem((layers, lats), F32),
+        vmem((layers, 1, lats), F32),
+        vmem((layers, dl, lats), BF),
+        vmem((pairs, dl, lats), BF),
         dma((4 + layers + pairs,)),
         dma((2, 2)),
         dma((2, 2)),
-        dma((2, na, 3)),
-        dma((2, na, 3)),
-        dma((2, nb, 3)),
-        dma((2, nb, 3)),
-        dma((2, ny)),
+        dma((2,)),
+        dma((2, na, tiles)),
+        dma((2, nb, tiles)),
         dma((2, ny)),
         dma((4, layers)),
         dma((4, layers)),
-        dma((2, 3)),
-        dma((na, 3)),
-        dma((na, 3)),
-        dma((nb, 3)),
-        dma((nb, 3)),
-        dma((2, 3)),
         dma((2,)),
+        dma((1,)),
+        dma((na, tiles)),
+        dma((nb, tiles)),
+        dma((1,)),
+        dma((tiles,)),
+        dma((2,)),
+        dma((layers + pairs,)),
     ]
     in_vmem = pl.BlockSpec(memory_space=pltpu.VMEM)
-    anywhere = pl.BlockSpec(memory_space=pl.ANY)
-    rec, eg, bg, dg = pl.pallas_call(
+    hbm = pl.BlockSpec(memory_space=pltpu.HBM)
+    made = pl.pallas_call(
         functools.partial(kernel, sizes),
         out_shape=(
-            jax.ShapeDtypeStruct((rows, width), BF),
+            jax.ShapeDtypeStruct((rows, layers, dl), BF),
             jax.ShapeDtypeStruct((layers, dl, lats), BF),
             jax.ShapeDtypeStruct((layers, lats), F32),
             jax.ShapeDtypeStruct((pairs, dl, lats), BF),
         ),
-        in_specs=[anywhere] * 6,
-        out_specs=(in_vmem,) * 4,
+        in_specs=[hbm] * 6,
+        out_specs=(in_vmem, hbm, in_vmem, hbm),
         scratch_shapes=scratch,
         compiler_params=pltpu.CompilerParams(
-            collective_id=0, has_side_effects=True, vmem_limit_bytes=60 * 1024 * 1024
+            collective_id=0, has_side_effects=True, vmem_limit_bytes=56 * 1024 * 1024
         ),
     )(
         layer_inputs.transpose(2, 0, 1),
@@ -593,7 +656,14 @@
         decoder,
         active_blocks.transpose(0, 2, 1),
     )
-    return rec.reshape(rows, layers, dl), eg, bg, dg
+    return pl.pallas_call(
+        hand_over,
+        out_shape=tuple(jax.ShapeDtypeStruct(v.shape, v.dtype) for v in made),
+        in_specs=[hbm] * 4,
+        out_specs=(hbm,) * 4,
+        scratch_shapes=[dma((layers + pairs + 2,))],
+        compiler_params=pltpu.CompilerParams(vmem_limit_bytes=56 * 1024 * 1024),
+    )(*made)
 
 
 def solution(mesh):

time: 112 us -> 156 us (1.39)
  Pallas kernels: 104 us -> 156 us
  local copies, waits for them, and re-layouts: 6.93 us -> 0 us
    pallas_call x0 -> x1, Pallas kernels: none -> 51.4 us  [step(): pl.pallas_call(hand_over, out_shape=tuple((jax.ShapeDtypeStruct(v.shape,...]
    unnamed x3 -> x0, local copies, waits for them, and re-layouts: 5.42 us -> none
where the time goes in v4:
time: 156 us
  Pallas kernels  156 us (100%)
    pallas_call x1, Pallas kernels, step(): pl.pallas_call(functools.partial(kernel, sizes), out_shape=(jax.ShapeDtyp...  104 us
    pallas_call x1, Pallas kernels, step(): pl.pallas_call(hand_over, out_shape=tuple((jax.ShapeDtypeStruct(v.shape,...  51.4 us

profile of v4, /device:TPU:1, one launch (start us, length us, event | category | flops | bytes accessed | tf_op | source)
XLA Modules:
  0.0 156.2 jit_solution(16874983525414165893)
XLA Ops:
  0.6 104.2 %shard_map.93 = (bf16[22,4,224]{2,1,0:T(4,128)(2,1)}, bf16[4,224,256]{2,1,0:T(8,128)(2,1)}, f32[4,256]{1,0:T(4,128)}, bf16[10,224,256]{2,1,0:T(8,128)(2,1)}) custom-call(bf16[22,4,224]{2,1,0:T(4,128)(2,1)} %bitcast.2, bf16[22,4,224]{2,1,0:T(4,128)(2,1)} %y_ref.1, bf16[4,224,256]{2,1,0:T(8,128)(2,1)} %enc_ref.1, f32[4,256]{1,0:T(4,128)} %bias_ref.1, ...), custom_call_target="tpu_custom_call" | custom-call | tf_op jit(solution)/shard_map/pallas_call | solution.py:637
  104.8 51.4 %shard_map.94 = (bf16[22,4,224]{2,1,0:T(4,128)(2,1)}, bf16[4,224,256]{2,1,0:T(8,128)(2,1)}, f32[4,256]{1,0:T(4,128)}, bf16[10,224,256]{2,1,0:T(8,128)(2,1)}) custom-call(bf16[22,4,224]{2,1,0:T(4,128)(2,1)} %get-tuple-element.8.refs_0_, bf16[4,224,256]{2,1,0:T(8,128)(2,1)} %get-tuple-element.9.refs_1_, f32[4,256]{1,0:T(4,128)} %get-tuple-element.10.refs_2_, ...), custom_call_target="tpu_custom_call" | custom-call | tf_op jit(solution)/shard_map/pallas_call | solution.py:659

commit v5 on v4

--- a/solution.py
+++ b/solution.py
@@ -28,7 +28,7 @@
     sizes,
     x_ref, y_ref, enc_ref, bias_ref, dec_ref, act_ref,
     rec_ref, eg_ref, bg_ref, dg_ref,
-    xg, eg, xt, et, cd, pgd, encp, dcat, sel, selt,
+    xg, eg, xt, et, cd, pgd, encp, dcat, dturn, sel, selt,
     xy_s, xy_r, pk, rx, ck, pc, rc, pg, slope,
     hm_s, hm_r, ho, ra_s, ra_r, rb_s, rb_r, fx_s, fx_r, recb, yc, x_in, y_in, act_in, bias_in, bsum, egb, dgb,
     load_sem, xy_out, xy_sem, ag_out, ag_ar, ag_br, ag_mr,
@@ -118,9 +118,6 @@
     pad = jnp.zeros((32 - rows, width), BF)
     loads[0].wait()
     xy_s[0] = jnp.concatenate([flat(x_in), pad], axis=0)
-    loads[1].wait()
-    xy_s[1] = jnp.concatenate([flat(y_in), pad], axis=0)
-
     pl.semaphore_wait(barrier, 5 + nl - 1)
 
     def xy_copy(n, to, w):
@@ -129,6 +126,10 @@
         )
 
     for n in range(2):
+        if n:
+            loads[1].wait()
+            xy_s[1] = jnp.concatenate([flat(y_in), pad], axis=0)
+
         @pl.when(owner)
         def _():
             xy_copy(n, partner, core).start()
@@ -279,16 +280,38 @@
     xg[own, :] = xy_arrive(0)
     loop(tiles, functools.partial(gather_start, x_copies))
 
-    gather_run(x_copies, [outputs])
+    def turn(src, out, lo, hi):
+        def one(n):
+            here = pl.ds(pl.multiple_of((n + lo) * LANE, LANE), LANE)
+            out[here, :] = src[:, here].T
+
+        loop(hi - lo, one)
+
+    def turn_part(src, out, i):
+        count = src.shape[1] // LANE
+        turn(src, out, count * i // na, count * (i + 1) // na)
+
+    for copy in dec_loads:
+        copy.wait()
+    gather_run(x_copies, [functools.partial(turn_part, dcat, dturn, i) for i in range(na)])
+    outputs()
     for copy in enc_loads:
         copy.wait()
 
     def lat_rows(j):
         return pl.ds(pl.multiple_of(j * shard, 16), shard)
 
+    nz = nl // 2
+
+    def peer_of(d):
+        j = (d - 1) // 2
+        away = nz // 2 + (j + 1) // 2 * (1 - 2 * lax.rem(j, 2))
+        there = lax.rem(q // nz + d, 2)
+        return there * nz + lax.rem(lax.rem(q, nz) + away, nz)
+
     def scatter(src, dst, s, n):
         def one(d, carry):
-            peer = lax.rem(q + d, nl)
+            peer = peer_of(d)
             pltpu.make_async_remote_copy(
                 src.at[s, lat_rows(peer)], dst.at[s, q], lat_s.at[n, s], lat_r.at[n, s],
                 device_id={"layer": me, "lat": peer},
@@ -302,7 +325,7 @@
         def one(d, carry):
             where = buf.at[s, lat_rows(q)]
             pltpu.make_async_remote_copy(
-                where, where, lat_s.at[n, s], lat_r.at[n, s], device_id={"layer": me, "lat": lax.rem(q + d, nl)}
+                where, where, lat_s.at[n, s], lat_r.at[n, s], device_id={"layer": me, "lat": peer_of(d)}
             ).start()
             return carry
 
@@ -328,15 +351,6 @@
         scatter(pk, rx, s, 0)
 
     loop(layers, encode)
-
-    def turn(src, out):
-        def one(n):
-            here = pl.ds(pl.multiple_of(n * LANE, LANE), LANE)
-            out[here, :] = src[:, here].T
-
-        loop(width // LANE, one)
-
-    turn(xg, xt)
 
     b_of = q * shard // SLOTS
     def activate(s):
@@ -368,9 +382,6 @@
 
     loop(layers, codes)
 
-    for copy in dec_loads:
-        copy.wait()
-
     groups = []
     for n in range(width // LANE):
         count = min(layers, ((n + 1) * LANE - 1) // dl + 1)
@@ -386,7 +397,7 @@
         base = pl.ds(pl.multiple_of(hh * half, TILE), half)
         for lo, hi, count in groups:
             lanes = slice(lo * LANE, hi * LANE)
-            ho[:, lanes] = dot(cd[base, 0 : count * lats], dcat[lanes, 0 : count * lats], ((1,), (1,)))
+            ho[:, lanes] = dot(cd[base, 0 : count * lats], dturn[0 : count * lats, lanes])
 
         @pl.when(j == 0)
         def _():
@@ -429,6 +440,7 @@
                 forward(b_copy, rb_s, rb_r, i, i - nb, c)
 
         loop(tiles, both)
+        turn_part(xg, xt, i)
 
     def fx_copy(c):
         here = small_tile(c)
@@ -482,7 +494,7 @@
         scatter(pc, rc, s, 2)
 
     loop(layers, back)
-    turn(eg, et)
+    turn(eg, et, 0, width // LANE)
 
     def decoder_grad(pair):
         t = jnp.int32(0)
@@ -494,7 +506,6 @@
         out_copy(dgb, dg_ref, pair, layers + pair).start()
 
     pairs = dg_ref.shape[0]
-    loop(pairs // 3, decoder_grad)
 
     def settle(s):
         lat_wait(lat_r, s, 2)
@@ -503,7 +514,21 @@
         spread(pg, s, 3)
 
     loop(layers, settle)
-    loop(pairs - pairs // 3, lambda n: decoder_grad(n + pairs // 3))
+    loop(pairs, decoder_grad)
+
+    @pl.when(owner)
+    def _():
+        rec_copy.wait_send()
+
+    @pl.when(jnp.logical_not(owner))
+    def _():
+        rec_copy.wait_recv()
+
+    take = jnp.where(iota((rows, chunk), 1) == iota((rows, chunk), 0) + rows * core, 1.0, 0.0).astype(BF)
+    out = dot(take, recb[...]).astype(BF)
+    for t in range(layers):
+        rec_ref[:, t, :] = out[:, t * dl : (t + 1) * dl]
+
 
     def encoder_grad(s):
         lat_wait(lat_r, s, 3)
@@ -518,19 +543,6 @@
     loop(layers, encoder_grad)
     for s in range(layers):
         bg_ref[s : s + 1, :] = bsum[s]
-
-    @pl.when(owner)
-    def _():
-        rec_copy.wait_send()
-
-    @pl.when(jnp.logical_not(owner))
-    def _():
-        rec_copy.wait_recv()
-
-    take = jnp.where(iota((rows, chunk), 1) == iota((rows, chunk), 0) + rows * core, 1.0, 0.0).astype(BF)
-    out = dot(take, recb[...]).astype(BF)
-    for t in range(layers):
-        rec_ref[:, t, :] = out[:, t * dl : (t + 1) * dl]
 
     for n in range(2):
         xy_copy(n, mate, core).wait_send()
@@ -552,19 +564,23 @@
 
 
 def hand_over(*refs):
-    count = (len(refs) - 1) // 2
-    sem = refs[-1]
+    count = (len(refs) - 2) // 3
+    come, go = refs[-2:]
     copies = []
     for n in range(count):
-        src, dst = refs[n], refs[count + n]
+        src, dst, mid = refs[n], refs[count + n], refs[2 * count + n]
         parts = src.shape[0] if n in (1, 3) else 1
         for p in range(parts):
-            pair = (src.at[p], dst.at[p]) if parts > 1 else (src, dst)
-            copies.append(pltpu.make_async_copy(*pair, sem.at[len(copies)]))
-    for copy in copies:
-        copy.start()
-    for copy in copies:
-        copy.wait()
+            a, b, c = (src.at[p], mid.at[p], dst.at[p]) if parts > 1 else (src, mid, dst)
+            k = len(copies)
+            copies.append((pltpu.make_async_copy(a, b, come.at[k]), pltpu.make_async_copy(b, c, go.at[k])))
+    for first, _ in copies:
+        first.start()
+    for first, second in copies:
+        first.wait()
+        second.start()
+    for _, second in copies:
+        second.wait()
 
 
 def step(sizes, layer_inputs, layer_outputs, encoder, encoder_bias, decoder, active_blocks):
@@ -585,6 +601,7 @@
         vmem((places, layers * lats), BF),
         vmem((layers, 3 * LANE, lats), BF),
         vmem((width, layers * lats), BF),
+        vmem((layers * lats, width), BF),
         vmem((layers, 2 * SLOTS, places), BF),
         vmem((layers, places, 2 * SLOTS), BF),
         vmem((2, 32, width), BF),
@@ -661,7 +678,7 @@
         out_shape=tuple(jax.ShapeDtypeStruct(v.shape, v.dtype) for v in made),
         in_specs=[hbm] * 4,
         out_specs=(hbm,) * 4,
-        scratch_shapes=[dma((layers + pairs + 2,))],
+        scratch_shapes=[vmem(v.shape, v.dtype) for v in made] + [dma((layers + pairs + 2,))] * 2,
         compiler_params=pltpu.CompilerParams(vmem_limit_bytes=56 * 1024 * 1024),
     )(*made)
 

time: 156 us -> 106 us (0.68)
  Pallas kernels: 156 us -> 105 us
    pallas_call x1, Pallas kernels: 51.4 us -> 2.43 us  [step(): pl.pallas_call(hand_over, out_shape=tuple((jax.ShapeDtypeStruct(v.shape,...]
where the time goes in v5:
time: 106 us
  Pallas kernels  105 us (99%)
    pallas_call x1, Pallas kernels, step(): pl.pallas_call(functools.partial(kernel, sizes), out_shape=(jax.ShapeDtyp...  103 us
    pallas_call x1, Pallas kernels, step(): pl.pallas_call(hand_over, out_shape=tuple((jax.ShapeDtypeStruct(v.shape,...  2.43 us

profile of v5, /device:TPU:1, one launch (start us, length us, event | category | flops | bytes accessed | tf_op | source)
XLA Modules:
  0.0 105.8 jit_solution(9635252672347391094)
XLA Ops:
  0.6 102.8 %shard_map.93 = (bf16[22,4,224]{2,1,0:T(4,128)(2,1)}, bf16[4,224,256]{2,1,0:T(8,128)(2,1)}, f32[4,256]{1,0:T(4,128)}, bf16[10,224,256]{2,1,0:T(8,128)(2,1)}) custom-call(bf16[22,4,224]{2,1,0:T(4,128)(2,1)} %bitcast.2, bf16[22,4,224]{2,1,0:T(4,128)(2,1)} %y_ref.1, bf16[4,224,256]{2,1,0:T(8,128)(2,1)} %enc_ref.1, f32[4,256]{1,0:T(4,128)} %bias_ref.1, ...), custom_call_target="tpu_custom_call" | custom-call | tf_op jit(solution)/shard_map/pallas_call | solution.py:654
  103.4 2.4 %shard_map.94 = (bf16[22,4,224]{2,1,0:T(4,128)(2,1)}, bf16[4,224,256]{2,1,0:T(8,128)(2,1)}, f32[4,256]{1,0:T(4,128)}, bf16[10,224,256]{2,1,0:T(8,128)(2,1)}) custom-call(bf16[22,4,224]{2,1,0:T(4,128)(2,1)} %get-tuple-element.8.refs_0_, bf16[4,224,256]{2,1,0:T(8,128)(2,1)} %get-tuple-element.9.refs_1_, f32[4,256]{1,0:T(4,128)} %get-tuple-element.10.refs_2_, ...), custom_call_target="tpu_custom_call" | custom-call | tf_op jit(solution)/shard_map/pallas_call | solution.py:676

commit v6 on v5

--- a/solution.py
+++ b/solution.py
@@ -32,7 +32,7 @@
     xy_s, xy_r, pk, rx, ck, pc, rc, pg, slope,
     hm_s, hm_r, ho, ra_s, ra_r, rb_s, rb_r, fx_s, fx_r, recb, yc, x_in, y_in, act_in, bias_in, bsum, egb, dgb,
     load_sem, xy_out, xy_sem, ag_out, ag_ar, ag_br, ag_mr,
-    lat_s, lat_r, hm_sem, rs_out, rs_ar, rs_br, fx_out, fx_sem, rec_sem, out_sem,
+    lat_s, lat_r, hm_out, hm_sem, rs_out, rs_ar, rs_br, fx_out, fx_sem, rec_sem, out_sem,
 ):
     layers, dl, lats, rows, ny, nl, chunk = sizes
     width = layers * dl
@@ -56,6 +56,9 @@
     mate, partner = at(h, y, 1 - core), at(1 - h, y, core)
     y_a, y_b = lax.rem(y + step + ny, ny), lax.rem(y - step + ny, ny)
     to_a, to_b = at(h, y_a, core), at(h, y_b, core)
+    two_a = at(h, lax.rem(y + 2 * step + ny, ny), core)
+    two_b = at(h, lax.rem(y - 2 * step + ny, ny), core)
+    stages = na - 1
 
     def place(hh, offset):
         slot = lax.rem(y + step * offset + 2 * ny, ny)
@@ -77,7 +80,7 @@
     diagonal = at(1 - h, y, 1 - core)
 
     barrier = pltpu.get_barrier_semaphore()
-    for peer in (mate, partner, diagonal, to_a, to_b):
+    for peer in (mate, partner, diagonal, to_a, to_b, two_a, two_b):
         pl.semaphore_signal(barrier, inc=1, device_id=peer)
 
     def greet(d, carry):
@@ -118,7 +121,7 @@
     pad = jnp.zeros((32 - rows, width), BF)
     loads[0].wait()
     xy_s[0] = jnp.concatenate([flat(x_in), pad], axis=0)
-    pl.semaphore_wait(barrier, 5 + nl - 1)
+    pl.semaphore_wait(barrier, 7 + nl - 1)
 
     def xy_copy(n, to, w):
         return pltpu.make_async_remote_copy(
@@ -169,6 +172,8 @@
             return pltpu.make_async_remote_copy(where, where, send, recv, device_id=to)
 
         def a_out(i, c):
+            if i == na - 1:
+                return piece(two_a, 2 - na, ag_out.at[n], ag_ar.at[n, i, c], c)
             return piece(to_a, -i, ag_out.at[n], ag_ar.at[n, i, c], c)
 
         def b_out(i, c):
@@ -186,8 +191,8 @@
             if i < nb:
                 order.append(i + 1)
 
-        def pass_on(j):
-            where = buf.at[place(core, order[j])]
+        def pass_on(j, c=None):
+            where = buf.at[place(core, order[j]) if c is None else tile_of(core, order[j], c)]
             return pltpu.make_async_remote_copy(where, where, ag_out.at[n], ag_mr.at[n, j], device_id=mate)
 
         def from_mate(j):
@@ -196,30 +201,39 @@
 
         return a_out, b_out, a_in, b_in, pass_on, from_mate
 
+    def start_a(copies, i, c):
+        copies[0](i, c).start()
+        if i == stages - 1:
+            copies[0](na - 1, c).start()
+
     def gather_start(copies, c):
-        copies[0](0, c).start()
-        if nb:
-            copies[1](0, c).start()
+        start_a(copies, 0, c)
+        copies[1](0, c).start()
 
     def gather_run(copies, extra):
         a_out, b_out, a_in, b_in, pass_on, from_mate = copies
         pass_on(0).start()
-        j = 1
-        for i in range(na):
+        for i in range(stages):
+            last = i + 1 == stages
 
             def advance(c):
                 a_in(i, c).wait_recv()
-                if i + 1 < na:
-                    a_out(i + 1, c).start()
-                if i < nb:
-                    b_in(i, c).wait_recv()
-                    if i + 1 < nb:
-                        b_out(i + 1, c).start()
+                if last:
+                    pass_on(2 * i + 1, c).start()
+                else:
+                    start_a(copies, i + 1, c)
+                b_in(i, c).wait_recv()
+                if last:
+                    pass_on(2 * i + 2, c).start()
+                    a_in(na - 1, c).wait_recv()
+                    pass_on(2 * i + 3, c).start()
+                else:
+                    b_out(i + 1, c).start()
 
             loop(tiles, advance)
-            for _ in range(2 if i < nb else 1):
-                pass_on(j).start()
-                j += 1
+            if not last:
+                pass_on(2 * i + 1).start()
+                pass_on(2 * i + 2).start()
             if i < len(extra):
                 extra[i]()
         for j in range(ny):
@@ -289,11 +303,11 @@
 
     def turn_part(src, out, i):
         count = src.shape[1] // LANE
-        turn(src, out, count * i // na, count * (i + 1) // na)
+        turn(src, out, count * i // stages, count * (i + 1) // stages)
 
     for copy in dec_loads:
         copy.wait()
-    gather_run(x_copies, [functools.partial(turn_part, dcat, dturn, i) for i in range(na)])
+    gather_run(x_copies, [functools.partial(turn_part, dcat, dturn, i) for i in range(stages)])
     outputs()
     for copy in enc_loads:
         copy.wait()
@@ -390,7 +404,16 @@
         else:
             groups.append([n, n + 1, count])
 
-    hm_copy = pltpu.make_async_remote_copy(hm_s, hm_r, hm_sem.at[0], hm_sem.at[1], device_id=mate)
+    uses = [na, na - 1, -nb]
+    for i in range(1, nb):
+        uses += [na - 1 - i, i - nb]
+    uses.append(0)
+
+    def hm_copy(offset, sign):
+        where = place(0, sign * offset)
+        return pltpu.make_async_remote_copy(
+            hm_s.at[where], hm_r.at[where], hm_out.at[0], hm_sem.at[uses.index(offset)], device_id=mate
+        )
 
     def decode(j):
         hh = jnp.where(j == 0, 1 - core, core)
@@ -402,10 +425,10 @@
         @pl.when(j == 0)
         def _():
             hm_s[...] = ho[...].astype(BF)
-            hm_copy.start()
+            for offset in uses:
+                hm_copy(offset, -1).start()
 
     loop(2, decode)
-    hm_copy.wait_recv()
 
     def mine(offset, c):
         where = tile_of(0, offset, c)
@@ -416,7 +439,11 @@
 
     def a_copy(i, c):
         return pltpu.make_async_remote_copy(
-            ra_s.at[i, small_tile(c)], ra_r.at[i, small_tile(c)], rs_out.at[0], rs_ar.at[i, c], device_id=to_a
+            ra_s.at[i, small_tile(c)],
+            ra_r.at[i, small_tile(c)],
+            rs_out.at[0],
+            rs_ar.at[i, c],
+            device_id=to_a if i else two_a,
         )
 
     def b_copy(i, c):
@@ -424,23 +451,32 @@
             rb_s.at[i, small_tile(c)], rb_r.at[i, small_tile(c)], rs_out.at[0], rs_br.at[i, c], device_id=to_b
         )
 
-    def forward(copy, buf_s, buf_r, i, offset, c):
+    def forward(copy, buf_s, buf_r, i, offset, earlier, c):
         part = mine(offset, c)
-        if i:
-            copy(i - 1, c).wait_recv()
-            part = part + buf_r[i - 1, small_tile(c), :].astype(F32)
+        for n in earlier:
+            copy(n, c).wait_recv()
+            part = part + buf_r[n, small_tile(c), :].astype(F32)
         buf_s[i, small_tile(c), :] = part.astype(BF)
         copy(i, c).start()
 
-    for i in range(na):
+    def from_a(i):
+        return [] if i < 2 else [0, 1] if i == 2 else [i - 1]
+
+    for i in range(stages):
+        now = [na, na - 1, -nb] if i == 0 else [na - 1 - i, i - nb]
+        for offset in now:
+            hm_copy(offset, 1).wait_recv()
 
         def both(c):
-            forward(a_copy, ra_s, ra_r, i, na - i, c)
-            if i < nb:
-                forward(b_copy, rb_s, rb_r, i, i - nb, c)
+            if i == 0:
+                forward(a_copy, ra_s, ra_r, 0, na, [], c)
+            forward(a_copy, ra_s, ra_r, i + 1, na - 1 - i, from_a(i + 1), c)
+            forward(b_copy, rb_s, rb_r, i, i - nb, [i - 1] if i else [], c)
 
         loop(tiles, both)
         turn_part(xg, xt, i)
+
+    hm_copy(0, 1).wait_recv()
 
     def fx_copy(c):
         here = small_tile(c)
@@ -451,11 +487,11 @@
     def finish(c):
         here = small_tile(c)
         total = mine(0, c)
-        a_copy(na - 1, c).wait_recv()
-        total = total + ra_r[na - 1, here, :].astype(F32)
-        if nb:
-            b_copy(nb - 1, c).wait_recv()
-            total = total + rb_r[nb - 1, here, :].astype(F32)
+        for n in from_a(na):
+            a_copy(n, c).wait_recv()
+            total = total + ra_r[n, here, :].astype(F32)
+        b_copy(nb - 1, c).wait_recv()
+        total = total + rb_r[nb - 1, here, :].astype(F32)
         fx_s[here, :] = total.astype(BF)
         fx_copy(c).start()
 
@@ -553,7 +589,7 @@
 
     loop(layers, lambda s: out_copy(egb, eg_ref, s, s).wait())
     loop(pairs, lambda n: out_copy(dgb, dg_ref, n, layers + n).wait())
-    hm_copy.wait_send()
+    sent(hm_s, half, hm_out.at[0])
     sent(xg, chunk, fx_out.at[0])
     sent(xg, (na + nb) * chunk, rs_out.at[0])
     for n in range(2):
@@ -640,7 +676,8 @@
         dma((2, ny)),
         dma((4, layers)),
         dma((4, layers)),
-        dma((2,)),
+        dma((1,)),
+        dma((ny,)),
         dma((1,)),
         dma((na, tiles)),
         dma((nb, tiles)),

time: 106 us -> 101 us (0.953)
  Pallas kernels: 105 us -> 99.9 us
    pallas_call x1, Pallas kernels: 103 us -> 97.4 us  [step(): pl.pallas_call(functools.partial(kernel, sizes), out_shape=(jax.ShapeDtyp...]
where the time goes in v6:
time: 101 us
  Pallas kernels  99.9 us (99%)
    pallas_call x1, Pallas kernels, step(): pl.pallas_call(functools.partial(kernel, sizes), out_shape=(jax.ShapeDtyp...  97.4 us
    pallas_call x1, Pallas kernels, step(): pl.pallas_call(hand_over, out_shape=tuple((jax.ShapeDtypeStruct(v.shape,...  2.43 us

profile of v6, /device:TPU:1, one launch (start us, length us, event | category | flops | bytes accessed | tf_op | source)
XLA Modules:
  0.0 100.5 jit_solution(13255033081321360631)
XLA Ops:
  0.6 97.4 %shard_map.93 = (bf16[22,4,224]{2,1,0:T(4,128)(2,1)}, bf16[4,224,256]{2,1,0:T(8,128)(2,1)}, f32[4,256]{1,0:T(4,128)}, bf16[10,224,256]{2,1,0:T(8,128)(2,1)}) custom-call(bf16[22,4,224]{2,1,0:T(4,128)(2,1)} %bitcast.2, bf16[22,4,224]{2,1,0:T(4,128)(2,1)} %y_ref.1, bf16[4,224,256]{2,1,0:T(8,128)(2,1)} %enc_ref.1, f32[4,256]{1,0:T(4,128)} %bias_ref.1, ...), custom_call_target="tpu_custom_call" | custom-call | tf_op jit(solution)/shard_map/pallas_call | solution.py:691
  98.1 2.4 %shard_map.94 = (bf16[22,4,224]{2,1,0:T(4,128)(2,1)}, bf16[4,224,256]{2,1,0:T(8,128)(2,1)}, f32[4,256]{1,0:T(4,128)}, bf16[10,224,256]{2,1,0:T(8,128)(2,1)}) custom-call(bf16[22,4,224]{2,1,0:T(4,128)(2,1)} %get-tuple-element.8.refs_0_, bf16[4,224,256]{2,1,0:T(8,128)(2,1)} %get-tuple-element.9.refs_1_, f32[4,256]{1,0:T(4,128)} %get-tuple-element.10.refs_2_, ...), custom_call_target="tpu_custom_call" | custom-call | tf_op jit(solution)/shard_map/pallas_call | solution.py:713

commit v7 on v6

--- a/solution.py
+++ b/solution.py
@@ -287,8 +287,6 @@
     def outputs():
         yc[...] = xy_arrive(1)
 
-    loop(layers, choose)
-
     own = place(core, 0)
     x_copies = gather_copies(xg, 0)
     xg[own, :] = xy_arrive(0)
@@ -305,9 +303,11 @@
         count = src.shape[1] // LANE
         turn(src, out, count * i // stages, count * (i + 1) // stages)
 
-    for copy in dec_loads:
-        copy.wait()
-    gather_run(x_copies, [functools.partial(turn_part, dcat, dturn, i) for i in range(stages)])
+    def choose_part(i):
+        lo, hi = layers * i // stages, layers * (i + 1) // stages
+        loop(hi - lo, lambda s: choose(s + lo))
+
+    gather_run(x_copies, [functools.partial(choose_part, i) for i in range(stages)])
     outputs()
     for copy in enc_loads:
         copy.wait()
@@ -365,6 +365,9 @@
         scatter(pk, rx, s, 0)
 
     loop(layers, encode)
+    for copy in dec_loads:
+        copy.wait()
+    turn(dcat, dturn, 0, layers * lats // LANE)
 
     b_of = q * shard // SLOTS
     def activate(s):
@@ -525,11 +528,13 @@
         return pltpu.make_async_copy(buf.at[n], ref.at[n], out_sem.at[sem])
 
     def back(s):
-        dense = dot(eg[...], dcat[:, lane_block(s)]).astype(BF)
+        low = dl * s // LANE * LANE
+        dense = dot(eg[:, low:width], dcat[low:width, s * lats : (s + 1) * lats]).astype(BF)
         pack(dense, pc, s)
         scatter(pc, rc, s, 2)
 
-    loop(layers, back)
+    for s in range(layers - 1, -1, -1):
+        back(s)
     turn(eg, et, 0, width // LANE)
 
     def decoder_grad(pair):
@@ -549,7 +554,7 @@
         pg[s, lat_rows(q), :] = (total * slope[s]).astype(BF)
         spread(pg, s, 3)
 
-    loop(layers, settle)
+    loop(layers, lambda i: settle(layers - 1 - i))
     loop(pairs, decoder_grad)
 
     @pl.when(owner)
@@ -576,7 +581,7 @@
         egb[s] = dot(xt[pl.ds(pl.multiple_of(s * dl, TILE), dl), :], pgd[:, lane_block(s)]).astype(BF)
         out_copy(egb, eg_ref, s, s).start()
 
-    loop(layers, encoder_grad)
+    loop(layers, lambda i: encoder_grad(layers - 1 - i))
     for s in range(layers):
         bg_ref[s : s + 1, :] = bsum[s]
 

time: 101 us -> 100 us (0.990)
  no operation moved by 1% of the time
where the time goes in v7:
time: 100 us
  Pallas kernels  99.5 us (100%)
    pallas_call x1, Pallas kernels, step(): pl.pallas_call(functools.partial(kernel, sizes), out_shape=(jax.ShapeDtyp...  97 us
    pallas_call x1, Pallas kernels, step(): pl.pallas_call(hand_over, out_shape=tuple((jax.ShapeDtypeStruct(v.shape,...  2.43 us

profile of v7, /device:TPU:1, one launch (start us, length us, event | category | flops | bytes accessed | tf_op | source)
XLA Modules:
  0.0 100.1 jit_solution(16336504594066657417)
XLA Ops:
  0.6 97.0 %shard_map.93 = (bf16[22,4,224]{2,1,0:T(4,128)(2,1)}, bf16[4,224,256]{2,1,0:T(8,128)(2,1)}, f32[4,256]{1,0:T(4,128)}, bf16[10,224,256]{2,1,0:T(8,128)(2,1)}) custom-call(bf16[22,4,224]{2,1,0:T(4,128)(2,1)} %bitcast.2, bf16[22,4,224]{2,1,0:T(4,128)(2,1)} %y_ref.1, bf16[4,224,256]{2,1,0:T(8,128)(2,1)} %enc_ref.1, f32[4,256]{1,0:T(4,128)} %bias_ref.1, ...), custom_call_target="tpu_custom_call" | custom-call | tf_op jit(solution)/shard_map/pallas_call | solution.py:696
  97.7 2.4 %shard_map.94 = (bf16[22,4,224]{2,1,0:T(4,128)(2,1)}, bf16[4,224,256]{2,1,0:T(8,128)(2,1)}, f32[4,256]{1,0:T(4,128)}, bf16[10,224,256]{2,1,0:T(8,128)(2,1)}) custom-call(bf16[22,4,224]{2,1,0:T(4,128)(2,1)} %get-tuple-element.8.refs_0_, bf16[4,224,256]{2,1,0:T(8,128)(2,1)} %get-tuple-element.9.refs_1_, f32[4,256]{1,0:T(4,128)} %get-tuple-element.10.refs_2_, ...), custom_call_target="tpu_custom_call" | custom-call | tf_op jit(solution)/shard_map/pallas_call | solution.py:718
